TPU v7x, 256 devices: a whole 4x4x8 slice. The times are simulated.
256 devices in a mesh: space: 16 (over z, y_hi), leaf: 16 (over x, y_lo, core).
Axes of the slice: x: 4, y: 4 (y_hi: 2, y_lo: 2; y = y_hi * 2 + y_lo), z: 8, core: 2. Of those that a mesh axis runs over, the one named last changes fastest.
Arguments:
- charges: bfloat16 [16, 2097152], P(None, ('space', 'leaf')), may hold values from -6 to 6
- leaf_basis: bfloat16 [16384, 64, 128], P(('space', 'leaf')), may hold values from -0.5 to 0.5
- transfer_one: bfloat16 [2048, 64, 512], P(('space', 'leaf')), may hold values from -0.25 to 0.25
- transfer_two: bfloat16 [256, 64, 512], P(('space', 'leaf')), may hold values from -0.25 to 0.25
- nodes_leaf: bfloat16 [16384, 3, 64], P(('space', 'leaf')), may hold values from 0 to 6
- nodes_one: bfloat16 [2048, 3, 64], P(('space', 'leaf')), may hold values from 0 to 6
- nodes_two: bfloat16 [256, 3, 64], P(('space', 'leaf')), may hold values from 0 to 6
- links_leaf: int32 [16384, 96], P(('space', 'leaf')), may hold values from -1 to 16383, as said below
- links_one: int32 [2048, 96], P(('space', 'leaf')), may hold values from -1 to 2047, as said below
- links_two: int32 [256, 96], P(('space', 'leaf')), may hold values from -1 to 255, as said below
Outputs:
- potentials: bfloat16 [16, 2097152], P(None, ('space', 'leaf'))
Inputs may be any that keep to these rules, and one draw needn't show every extreme that they name: `links_leaf`: A live source leaf lies on a device whose space index differs from that of the target leaf's device by at most one; live slots of a row come first. `links_one`: A live source cluster lies on a device whose space index differs from that of the target's device by at most one; live slots of a row come first. `links_two`: live slots of a row come first.
All inputs are finite; a program needn't handle non-finite values.
Results may differ from a plain program's by a relative error of at most 0.007.
Values may be sent and summed in bfloat16 or wider, within the bound.
A program may use at most 128 MiB of HBM per device.

v0:
```python
import jax
import jax.numpy as jnp
from jax import lax
from jax.sharding import PartitionSpec as P

SQRT_THREE = 1.7320508075688772
LENGTH = 2.0
AMPLITUDE = 0.25


def with_halo(cells, sides, width):
    for axis, dim in sides:
        count = lax.axis_size(axis)
        ends = count - 1
        head = lax.slice_in_dim(cells, 0, width, axis=dim)
        tail = lax.slice_in_dim(cells, cells.shape[dim] - width, cells.shape[dim], axis=dim)
        cells = jnp.concatenate(
            [
                lax.ppermute(tail, axis, [(i, (i + 1) % count) for i in range(ends)]),
                cells,
                lax.ppermute(head, axis, [((i + 1) % count, i) for i in range(ends)]),
            ],
            axis=dim,
        )
    return cells


def matern_block(target_nodes, source_nodes):
    diff = target_nodes[:, None, :, :, None] - source_nodes[:, :, :, None, :]
    dist = jnp.sqrt(jnp.sum(diff * diff, axis=2)) * (SQRT_THREE / LENGTH)
    return (AMPLITUDE * (1.0 + dist) * jnp.exp(-dist)).astype(jnp.bfloat16)


def couple(table_coef, table_nodes, rows, live, target_nodes, rank, width):
    count = rows.shape[0]
    slots = rows.shape[1]
    group = min(count, 4)

    def one_group(args):
        index, alive, tnodes = args
        picked = table_coef[index].reshape(group, slots, rank, width)
        picked = jnp.where(alive[:, :, None, None], picked, jnp.zeros((), jnp.bfloat16))
        source_nodes = table_nodes[index].astype(jnp.float32)
        matrix = matern_block(tnodes.astype(jnp.float32), source_nodes)
        return jnp.einsum("gjab,gjbv->gav", matrix, picked, preferred_element_type=jnp.float32)

    result = lax.map(
        one_group,
        (
            rows.reshape(-1, group, slots),
            live.reshape(-1, group, slots),
            target_nodes.reshape(-1, group, 3, rank),
        ),
    )
    return result.reshape(count, rank, width)


def local(
    charges,
    leaf_basis,
    transfer_one,
    transfer_two,
    nodes_leaf,
    nodes_one,
    nodes_two,
    links_leaf,
    links_one,
    links_two,
):
    width = charges.shape[0]
    leaf_dev = leaf_basis.shape[0]
    rank = leaf_basis.shape[1]
    leaf_size = leaf_basis.shape[2]
    one_dev = leaf_dev // 8
    two_dev = one_dev // 8
    n_leaf = lax.axis_size("leaf")
    my_space = lax.axis_index("space")
    shaped = charges.reshape(width, leaf_dev, leaf_size)
    coef_leaf = jnp.einsum(
        "tkp,vtp->tkv", leaf_basis, shaped, preferred_element_type=jnp.float32
    ).astype(jnp.bfloat16)
    coef_one = jnp.einsum(
        "pkm,pmv->pkv",
        transfer_one,
        coef_leaf.reshape(one_dev, 8 * rank, width),
        preferred_element_type=jnp.float32,
    ).astype(jnp.bfloat16)
    coef_two = jnp.einsum(
        "pkm,pmv->pkv",
        transfer_two,
        coef_one.reshape(two_dev, 8 * rank, width),
        preferred_element_type=jnp.float32,
    ).astype(jnp.bfloat16)
    flat_leaf = coef_leaf.reshape(leaf_dev, rank * width)
    whole_coef, whole_nodes = (
        lax.all_gather(flat_leaf, "leaf", axis=0, tiled=True),
        lax.all_gather(nodes_leaf, "leaf", axis=0, tiled=True),
    )
    near_coef, near_nodes = (
        with_halo(whole_coef[None], (("space", 0),), 1),
        with_halo(whole_nodes[None], (("space", 0),), 1),
    )
    live_leaf = links_leaf >= 0
    safe_leaf = jnp.where(live_leaf, links_leaf, 0)
    owner = safe_leaf // leaf_dev
    rows_leaf = (
        (owner // n_leaf - my_space + 1) * (n_leaf * leaf_dev)
        + owner % n_leaf * leaf_dev
        + safe_leaf % leaf_dev
    )
    rows_leaf = jnp.where(live_leaf, rows_leaf, 0)
    far_leaf = couple(
        near_coef.reshape(-1, rank * width),
        near_nodes.reshape(-1, 3, rank),
        rows_leaf,
        live_leaf,
        nodes_leaf,
        rank,
        width,
    )
    flat_one = coef_one.reshape(one_dev, rank * width)
    block_coef, block_nodes = (
        lax.all_gather(flat_one, "leaf", axis=0, tiled=True),
        lax.all_gather(nodes_one, "leaf", axis=0, tiled=True),
    )
    band_coef, band_nodes = (
        with_halo(block_coef[None], (("space", 0),), 1),
        with_halo(block_nodes[None], (("space", 0),), 1),
    )
    live_one = links_one >= 0
    safe_one = jnp.where(live_one, links_one, 0)
    owner_one = safe_one // one_dev
    rows_one = (
        (owner_one // n_leaf - my_space + 1) * (n_leaf * one_dev)
        + owner_one % n_leaf * one_dev
        + safe_one % one_dev
    )
    rows_one = jnp.where(live_one, rows_one, 0)
    far_one = couple(
        band_coef.reshape(-1, rank * width),
        band_nodes.reshape(-1, 3, rank),
        rows_one,
        live_one,
        nodes_one,
        rank,
        width,
    )
    flat_two = coef_two.reshape(two_dev, rank * width)
    every_coef, every_nodes = (
        lax.all_gather(flat_two, ("space", "leaf"), axis=0, tiled=True),
        lax.all_gather(nodes_two, ("space", "leaf"), axis=0, tiled=True),
    )
    live_two = links_two >= 0
    rows_two = jnp.where(live_two, links_two, 0)
    far_two = couple(every_coef, every_nodes, rows_two, live_two, nodes_two, rank, width)
    local_two = far_two.astype(jnp.bfloat16)
    down_one = jnp.einsum(
        "pkm,pkv->pmv", transfer_two, local_two, preferred_element_type=jnp.float32
    )
    local_one = (far_one + down_one.reshape(one_dev, rank, width)).astype(jnp.bfloat16)
    down_leaf = jnp.einsum(
        "pkm,pkv->pmv", transfer_one, local_one, preferred_element_type=jnp.float32
    )
    local_leaf = (far_leaf + down_leaf.reshape(leaf_dev, rank, width)).astype(jnp.bfloat16)
    result = jnp.einsum("tkp,tkv->vtp", leaf_basis, local_leaf, preferred_element_type=jnp.float32)
    return result.reshape(width, leaf_dev * leaf_size).astype(jnp.bfloat16)


def solution(mesh):
    return jax.shard_map(
        local,
        mesh=mesh,
        in_specs=(
            P(None, ("space", "leaf")),
            P(("space", "leaf"), None, None),
            P(("space", "leaf"), None, None),
            P(("space", "leaf"), None, None),
            P(("space", "leaf"), None, None),
            P(("space", "leaf"), None, None),
            P(("space", "leaf"), None, None),
            P(("space", "leaf"), None),
            P(("space", "leaf"), None),
            P(("space", "leaf"), None),
        ),
        out_specs=P(None, ("space", "leaf")),
        check_vma=False,
    )
```

profile of v0, /device:TPU:137, one launch (start us, length us, event | category | flops | bytes accessed | tf_op | source)
XLA Modules:
  0.0 1369.0 jit_solution(4095242045511093542)
XLA Ops:
  10.6 17.4 %all_gather.20 = bf16[128,3,64]{2,0,1:T(8,128)(2,1)S(1)} all-gather(bf16[8,3,64]{2,0,1:T(8,128)(2,1)} %param.19), channel_id=1, replica_groups=mesh['space'=16,'leaf'=16] {'leaf'}, dimensions={0}, use_global_device_ids=true | all-gather | bytes 52224 | tf_op jit(solution)/shard_map/all_gather | solution.py:124
  36.7 21.0 %all_gather.21 = bf16[128,1024]{1,0:T(8,128)(2,1)S(1)} all-gather(bf16[8,1024]{1,0:T(8,128)(2,1)S(1)} %reshape.238), channel_id=1, replica_groups=mesh['space'=16,'leaf'=16] {'leaf'}, dimensions={0}, use_global_device_ids=true | all-gather | bytes 278528 | tf_op jit(solution)/shard_map/all_gather | solution.py:123
  66.1 26.5 %all_gather.18 = bf16[1024,3,64]{2,1,0:T(4,128)(2,1)S(1)} all-gather(bf16[64,3,64]{2,1,0:T(4,128)(2,1)S(1)} %copy.244), channel_id=1, replica_groups=mesh['space'=16,'leaf'=16] {'leaf'}, dimensions={0}, use_global_device_ids=true | all-gather | bytes 417792 | tf_op jit(solution)/shard_map/all_gather | solution.py:97
  95.8 340.5 %all_gather.22 = bf16[256,3,64]{2,1,0:T(4,128)(2,1)S(1)} all-gather(bf16[1,3,64]{2,1,0:T(4,128)(2,1)S(1)} %copy-done.10), channel_id=1, replica_groups=mesh['space'=16,'leaf'=16] {'space','leaf'}, dimensions={0}, use_global_device_ids=true | all-gather | bytes 98688 | tf_op jit(solution)/shard_map/all_gather | solution.py:151
  437.6 349.1 %all-gather = bf16[256,1,1024]{2,1,0:T(2,128)(2,1)S(1)} all-gather(bf16[1,1,1024]{2,1,0:T(2,128)(2,1)S(1)} %reshape.311), channel_id=1, replica_groups=mesh['space'=16,'leaf'=16] {'space','leaf'}, dimensions={0}, use_global_device_ids=true | all-gather | bytes 526336 | tf_op jit(solution)/shard_map/all_gather | solution.py:150
  797.6 7.0 collective-permute-start.3
  806.5 70.0 %while.25 = (s32[]{:T(128)}, f32[2,4,64,16]{2,3,1,0:T(8,128)}, bf16[2,4,3,64]{3,2,1,0:T(4,128)(2,1)S(1)}, s32[2,4,96]{2,1,0:T(4,128)S(1)}, bf16[384,3,64]{2,1,0:...) while((s32[]{:T(128)}, f32[2,4,64,16]{2,3,1,0:T(8,128)}, ...), condition=%wide.region_5.6_spmd, body=%wide.region_3.5_spmd.sunk | while | flops 72747904 | bytes 27565348 | solution.py:47
  819.4 6.5 multiply_reduce_fusion.6
  825.9 7.7 multiply_convert_fusion.6
  840.4 5.7 fusion.78
  849.1 6.5 multiply_reduce_fusion.6
  855.6 7.7 multiply_convert_fusion.6
  870.1 5.7 fusion.78
  887.6 12.3 collective-permute-done.3
  905.5 453.9 %while.24 = (s32[]{:T(128)}, f32[16,4,64,16]{2,1,0,3:T(4,128)}, bf16[16,4,3,64]{3,2,1,0:T(4,128)(2,1)S(1)}, s32[16,4,96]{2,1,0:T(4,128)}, bf16[3072,3,64]{2,1,0:...) while((s32[]{:T(128)}, f32[16,4,64,16]{2,1,0,3:T(4,128)}, ...), condition=%wide.region_2.3_spmd, body=%wide.region_0.2_spmd.sunk | while | flops 72747904 | bytes 27270436 | solution.py:47
  919.0 6.4 gather_fusion.1
  947.4 6.4 gather_fusion.1
  975.8 6.4 gather_fusion.1
  1004.2 6.4 gather_fusion.1
  1012.6 5.7 fusion.75
  1032.6 6.4 gather_fusion.1
  1061.0 6.4 gather_fusion.1
  1089.3 6.4 gather_fusion.1
  1117.6 6.4 gather_fusion.1
  1146.0 6.4 gather_fusion.1
  1174.4 6.4 gather_fusion.1
  1202.8 6.4 gather_fusion.1
  1231.1 6.4 gather_fusion.1
  1259.5 6.4 gather_fusion.1
  1287.8 6.4 gather_fusion.1
  1316.2 6.4 gather_fusion.1
  1344.6 6.4 gather_fusion.1
  (399 shorter events, 422.0 us)
Async XLA Ops:
  6.5 89.3 %copy-start.10 = (bf16[1,3,64]{2,1,0:T(4,128)(2,1)S(1)}, bf16[1,3,64]{2,1,0:T(4,128)(2,1)}, u32[]{:S(2)}) copy-start(bf16[1,3,64]{2,1,0:T(4,128)(2,1)} %param.20) | copy-start | bytes 1156
  6.5 429.8 %copy-start.11 = (s32[1,96]{1,0:T(1,128)S(1)}, s32[1,96]{1,0:T(1,128)}, u32[]{:S(2)}) copy-start(s32[1,96]{1,0:T(1,128)} %param.23) | copy-start | bytes 1156
  6.5 430.7 %copy-start.5 = (bf16[1,64,512]{2,1,0:T(8,128)(2,1)S(1)}, bf16[1,64,512]{2,1,0:T(8,128)(2,1)}, u32[]{:S(2)}) copy-start(bf16[1,64,512]{2,1,0:T(8,128)(2,1)} %param.17) | copy-start | bytes 196612
  6.5 791.0 %all-gather.3.cloned.1.call-start = ((), (), s32[]{:S(2)}) async-start(), calls=%async_computation | async-start | bytes 2228224 | tf_op jit(solution)/shard_map/all_gather | solution.py:96
  9.3 778.5 %copy-start.9 = (s32[8,96]{1,0:T(8,128)S(1)}, s32[8,96]{1,0:T(8,128)}, u32[]{:S(2)}) copy-start(s32[8,96]{1,0:T(8,128)} %param.22) | copy-start | bytes 9220
  9.3 779.1 %copy-start.6 = (s32[64,96]{1,0:T(8,128)S(1)}, s32[64,96]{1,0:T(8,128)}, u32[]{:S(2)}) copy-start(s32[64,96]{1,0:T(8,128)} %param.21) | copy-start | bytes 73732
  28.0 765.2 %collective-permute-start.5 = (bf16[1,128,3,64]{3,1,2,0:T(8,128)(2,1)S(1)}, bf16[1,128,3,64]{3,1,2,0:T(8,128)(2,1)}, u32[]{:S(2)}, u32[]{:S(2)}) collective-permute-start(bf16[1,128,3,64]{3,1,2,0:T(8,128)(2,1)S(1)} %bitcast.156), channel_id=1, source_target_pairs={{16,0},{32,16},{48,32},{64,48},{80,64},{96,80},{112,96},{128,112},... | collective-permute-start | bytes 147464 | tf_op jit(solution)/shard_map/ppermute | solution.py:21
  31.8 763.3 %collective-permute-start.4 = (bf16[1,128,3,64]{3,1,2,0:T(8,128)(2,1)S(1)}, bf16[1,128,3,64]{3,1,2,0:T(8,128)(2,1)}, u32[]{:S(2)}, u32[]{:S(2)}) collective-permute-start(bf16[1,128,3,64]{3,1,2,0:T(8,128)(2,1)S(1)} %bitcast.157), channel_id=1, source_target_pairs={{0,16},{16,32},{32,48},{48,64},{64,80},{80,96},{96,112},{112,128},... | collective-permute-start | bytes 147464 | tf_op jit(solution)/shard_map/ppermute | solution.py:19
  57.7 738.7 %collective-permute-start.7 = (bf16[1,128,1024]{2,1,0:T(8,128)(2,1)S(1)}, bf16[1,128,1024]{2,1,0:T(8,128)(2,1)}, u32[]{:S(2)}, u32[]{:S(2)}) collective-permute-start(bf16[1,128,1024]{2,1,0:T(8,128)(2,1)S(1)} %bitcast.151), channel_id=1, source_target_pairs={{16,0},{32,16},{48,32},{64,48},{80,64},{96,80},{112,96},{128,112},... | collective-permute-start | bytes 786440 | tf_op jit(solution)/shard_map/ppermute | solution.py:21
  63.3 733.1 %collective-permute-start.6 = (bf16[1,128,1024]{2,1,0:T(8,128)(2,1)S(1)}, bf16[1,128,1024]{2,1,0:T(8,128)(2,1)}, u32[]{:S(2)}, u32[]{:S(2)}) collective-permute-start(bf16[1,128,1024]{2,1,0:T(8,128)(2,1)S(1)} %bitcast.152), channel_id=1, source_target_pairs={{0,16},{16,32},{32,48},{48,64},{64,80},{80,96},{96,112},{112,128},... | collective-permute-start | bytes 786440 | tf_op jit(solution)/shard_map/ppermute | solution.py:19
  92.6 699.0 %copy-start.1 = (bf16[1024,3,64]{2,1,0:T(4,128)(2,1)}, bf16[1024,3,64]{2,1,0:T(4,128)(2,1)S(1)}, u32[]{:S(2)}) copy-start(bf16[1024,3,64]{2,1,0:T(4,128)(2,1)S(1)} %all_gather.18) | copy-start | bytes 1179652
  93.8 785.2 %collective-permute-start.1 = (bf16[1,1024,3,64]{1,3,2,0:T(8,128)(2,1)}, bf16[1,1024,3,64]{1,3,2,0:T(8,128)(2,1)}, u32[]{:S(2)}, u32[]{:S(2)}) collective-permute-start(bf16[1,1024,3,64]{1,3,2,0:T(8,128)(2,1)} %copy.246), channel_id=1, source_target_pairs={{16,0},{32,16},{48,32},{64,48},{80,64},{96,80},{112,96},{128,112},... | collective-permute-start | bytes 1179656 | tf_op jit(solution)/shard_map/ppermute | solution.py:21
  793.2 87.4 %collective-permute-start = (bf16[1,1024,3,64]{1,3,2,0:T(8,128)(2,1)}, bf16[1,1024,3,64]{1,3,2,0:T(8,128)(2,1)}, u32[]{:S(2)}, u32[]{:S(2)}) collective-permute-start(bf16[1,1024,3,64]{1,3,2,0:T(8,128)(2,1)} %copy.246), channel_id=1, source_target_pairs={{0,16},{16,32},{32,48},{48,64},{64,80},{80,96},{96,112},{112,128},... | collective-permute-start | bytes 1179656 | tf_op jit(solution)/shard_map/ppermute | solution.py:19
  797.6 102.4 %collective-permute-start.3 = (bf16[1,1024,1024]{2,1,0:T(8,128)(2,1)}, bf16[1,1024,1024]{2,1,0:T(8,128)(2,1)}, u32[]{:S(2)}, u32[]{:S(2)}) collective-permute-start(bf16[1,1024,1024]{2,1,0:T(8,128)(2,1)} %bitcast.147), channel_id=1, source_target_pairs={{16,0},{32,16},{48,32},{64,48},{80,64},{96,80},{112,96},{128,112},... | collective-permute-start | bytes 6291464 | tf_op jit(solution)/shard_map/ppermute | solution.py:21
  804.5 95.4 %collective-permute-start.2 = (bf16[1,1024,1024]{2,1,0:T(8,128)(2,1)}, bf16[1,1024,1024]{2,1,0:T(8,128)(2,1)}, u32[]{:S(2)}, u32[]{:S(2)}) collective-permute-start(bf16[1,1024,1024]{2,1,0:T(8,128)(2,1)} %bitcast.148), channel_id=1, source_target_pairs={{0,16},{16,32},{32,48},{48,64},{64,80},{80,96},{96,112},{112,128},... | collective-permute-start | bytes 6291464 | tf_op jit(solution)/shard_map/ppermute | solution.py:19
  882.2 17.7 %copy-start.2 = (bf16[1024,1024]{1,0:T(8,128)(2,1)S(1)}, bf16[1024,1024]{1,0:T(8,128)(2,1)}, u32[]{:S(2)}) copy-start(bf16[1024,1024]{1,0:T(8,128)(2,1)} %all-gather.3.cloned.1.call-done) | copy-start | bytes 6291460
  925.4 8.4 copy-start.4
  953.8 8.5 copy-start.4
  982.2 8.5 copy-start.4
  1010.6 8.4 copy-start.4
  1038.9 8.5 copy-start.4
  1067.3 8.4 copy-start.4
  1095.7 8.4 copy-start.4
  1124.0 8.5 copy-start.4
  1152.4 8.5 copy-start.4
  1180.8 8.4 copy-start.4
  1209.1 8.4 copy-start.4
  1237.5 8.4 copy-start.4
  1265.8 8.4 copy-start.4
  1294.1 8.5 copy-start.4
  1322.6 8.5 copy-start.4
  1351.0 8.4 copy-start.4
  (21 other events, 78.6 us)
Sparse Core Ops, SparseCore 0:
  10.7 40.2 all-gather.2
where the time goes:
time: 1380 us; the launch traced here: 1370 us
  blocking collectives  755 us (55%)
  local copies, waits for them, and re-layouts  224 us (16%)
  other arithmetic  216 us (16%)
  matrix products  109 us (8%)
  starting transfers between devices  27 us (2%)
  between operations  14.1 us (1%)
    all_gather x1, blocking collectives, local(): lax.all_gather(flat_two, ('space', 'leaf'), axis=0, tiled=True)  349 us
    all_gather x1, blocking collectives, local(): lax.all_gather(nodes_two, ('space', 'leaf'), axis=0, tiled=True)  341 us
    gather x38, local copies, waits for them, and re-layouts, one_group(): picked = table_coef[index].reshape(group, slots, rank, width)  115 us
    dot_general x19, matrix products, one_group(): jnp.einsum('gjab,gjbv->gav', matrix, picked, preferred_element_type=jnp.f...  104 us
    convert_element_type x19, other arithmetic, matern_block(): return (AMPLITUDE * (1.0 + dist) * jnp.exp(-dist)).astype(jnp.bfloat16)  103 us
    reduce_sum x19, other arithmetic, matern_block(): dist = jnp.sqrt(jnp.sum(diff * diff, axis=2)) * (SQRT_THREE / LENGTH)  66.6 us
    gather x20, local copies, waits for them, and re-layouts, one_group(): source_nodes = table_nodes[index].astype(jnp.float32)  54.8 us
  transfers between devices with their start and end apart: 9, of which 1 were waited for; matrix products, arithmetic and copies ran while one was open for 6% of the time, Pallas kernels for 0%

commit v1 on v0

v1 whole, which is shorter than its diff:
```python
import functools

import jax
import jax.numpy as jnp
from jax import lax
from jax.experimental import pallas as pl
from jax.experimental.pallas import tpu as pltpu
from jax.sharding import PartitionSpec as P

SCALE = 1.7320508075688772 / 2.0
AMPLITUDE = 0.25
LOG2E = 1.4426950408889634
MESH = pl.DeviceIdType.MESH
F32 = jnp.float32
BF16 = jnp.bfloat16

RANK = 64
LEAF_DEV = 64
ONE_DEV = 8
PAIRS = 37
PLANE = 48
ROWS = 80
SLOT = 72
TWO_AT = 12 * SLOT
ZERO_AT = TWO_AT + 64
ENTRIES = ZERO_AT + 8
UNROLL = 32

DIRECT = ((0, 1), (1, 0), (1, 1), (-1, 0), (-1, 1))


def nt(a, b):
    return lax.dot_general(a, b, (((1,), (1,)), ((), ())), preferred_element_type=F32)


def split3(value):
    first = value.astype(BF16).astype(F32)
    rest = value - first
    second = rest.astype(BF16).astype(F32)
    return first, second, rest - second


def up_kernel(
    n_space,
    charges, basis, t_one, t_two, nodes, links,
    node_tab, coef_tab, two_tab, target_nodes, lists,
    coef, entry, packed, order, value,
    local_sem, send_n, send_c, send_o, recv_n, recv_c, recv_o,
    send_e, recv_e, send_b, recv_b, send_x, recv_x, send_l, recv_l,
):
    space = lax.axis_index("space")
    leaf = lax.axis_index("leaf")
    x = leaf // 4
    four = lax.rem(leaf, 4)
    y_lo = four // 2
    core = lax.rem(four, 2)
    other_y = x * 4 + (1 - y_lo) * 2 + core
    sibling = x * 4 + y_lo * 2 + (1 - core)
    four_y = (1 - y_lo) * 2 + core
    has_prev = space > 0
    has_next = space < n_space - 1

    barrier = pltpu.get_barrier_semaphore()

    def greet(s, l):
        pl.semaphore_signal(barrier, inc=1, device_id=(s, l), device_id_type=MESH)

    for k in range(1, 4):
        greet(space, lax.rem(x + k, 4) * 4 + four)
    for k in range(1, n_space):
        greet(lax.rem(space + k, n_space), leaf)
    greet(space, other_y)
    greet(space, sibling)

    @pl.when(has_next)
    def _():
        greet(space + 1, other_y)

    @pl.when(has_prev)
    def _():
        greet(space - 1, other_y)

    def leaves(i, carry):
        for j in range(4):
            pair = i * 4 + j
            halves = [
                nt(charges[:, pl.ds(pl.multiple_of((2 * pair + h) * 128, 128), 128)], basis[2 * pair + h])
                for h in range(2)
            ]
            coef[pair] = jnp.concatenate(halves, axis=1).astype(BF16)
        return carry

    lax.fori_loop(0, 8, leaves, 0)

    neighbours = has_prev.astype(jnp.int32) + has_next.astype(jnp.int32)
    pl.semaphore_wait(barrier, 3 + (n_space - 1) + 2 + neighbours)

    def guarded(delta):
        if delta == 0:
            return lambda f: f()
        return pl.when(has_next if delta > 0 else has_prev)

    def remote(src, dst, send, recv, s, l):
        return pltpu.make_async_remote_copy(
            src_ref=src, dst_ref=dst, send_sem=send, recv_sem=recv, device_id=(s, l), device_id_type=MESH
        )

    LEAF_PART = pl.ds(0, 32)
    ONE_PART = pl.ds(32, 4)
    mine = 4 + four

    def node_copy(src, slot, k, s, l):
        return remote(src, node_tab.at[slot], send_n.at[k], recv_n.at[slot], s, l)

    def leaf_copy(src, slot, k, s, l):
        return remote(src, coef_tab.at[slot, LEAF_PART], send_c.at[k], recv_c.at[slot], s, l)

    def one_copy(src, slot, k, s, l):
        return remote(src, coef_tab.at[slot, ONE_PART], send_o.at[k], recv_o.at[slot], s, l)

    def place(delta, flip):
        return space + delta, (other_y if flip else leaf)

    def direct(make, src):
        for k, (delta, flip) in enumerate(DIRECT):
            @guarded(delta)
            def _(k=k, delta=delta, flip=flip):
                make(src, (1 - delta) * 4 + four, k, *place(delta, flip)).start()
        make(src, mine, 5, space, sibling).start()

    direct(leaf_copy, coef.at[LEAF_PART])
    direct(node_copy, nodes)
    for k in range(1, 4):
        to = lax.rem(x + k, 4) * 4 + four
        remote(nodes, target_nodes.at[x], send_x.at[k], recv_x.at[x], space, to).start()

    for i in range(4):
        halves = []
        for h in range(2):
            p = 2 * i + h
            stacked = jnp.concatenate([coef[4 * p + j] for j in range(4)], axis=1)
            halves.append(nt(stacked, t_one[p]))
        coef[32 + i] = jnp.concatenate(halves, axis=1).astype(BF16)
    direct(one_copy, coef.at[ONE_PART])

    top = nt(jnp.concatenate([coef[32 + j] for j in range(4)], axis=1), t_two[0])
    tile = nodes[32:48].astype(F32), nodes[80:96].astype(F32), nodes[128:144].astype(F32)
    tx, ty, tz = (part[4:5, :RANK] for part in tile)
    parts = (tx, ty, tz) + split3(tx * tx + ty * ty + tz * tz)
    row = lax.broadcasted_iota(jnp.int32, (16, RANK), 0)
    feature = jnp.where((row >= 6) & (row < 9), 1.0, 0.0)
    for k, part in enumerate(parts):
        feature = jnp.where(row == k, jnp.broadcast_to(part, (16, RANK)), feature)
    entry[...] = jnp.concatenate([feature, top], axis=1).astype(BF16)

    own_two = four * n_space + space

    def two_copy(k):
        return remote(
            entry, two_tab.at[own_two], send_e.at[k], recv_e.at[space],
            lax.rem(space + k, n_space), leaf,
        )

    for k in range(1, n_space):
        two_copy(k).start()
    keep_two = pltpu.make_async_copy(entry, two_tab.at[own_two], local_sem.at[0])
    keep_two.start()

    keeps = [
        pltpu.make_async_copy(nodes, node_tab.at[mine], local_sem.at[1]),
        pltpu.make_async_copy(coef.at[pl.ds(0, 36)], coef_tab.at[mine], local_sem.at[2]),
        pltpu.make_async_copy(nodes, target_nodes.at[x], local_sem.at[3]),
    ]
    for keep in keeps:
        keep.start()

    code = links[...]
    group = code // 1024
    entry_of = code - group * 1024
    before = jnp.where(
        lax.broadcasted_iota(jnp.int32, (128, 128), 0) < lax.broadcasted_iota(jnp.int32, (128, 128), 1), 1.0, 0.0
    ).astype(BF16)
    at = jnp.full((ROWS, 128), -1.0, F32)
    counts = []
    for q in range(4):
        member = jnp.where(group == q, 1.0, 0.0)
        rank = jnp.dot(member.astype(BF16), before, preferred_element_type=F32)
        at = jnp.where(group == q, rank + 128.0 * q, at)
        counts.append(jnp.sum(member, axis=1, keepdims=True))
    order[...] = at
    value[...] = entry_of.astype(F32)
    lane = lax.broadcasted_iota(jnp.int32, (8, 128), 1)
    lane_f = lane.astype(F32)
    for q in range(4):
        packed[q] = jnp.broadcast_to(jnp.maximum((counts[q].astype(jnp.int32) + 3) // 4, 1), (ROWS, 128))

    def compact(b, carry):
        rows = pl.ds(pl.multiple_of(b * 8, 8), 8)
        where = order[rows, :]
        what = value[rows, :]
        found = [jnp.full((8, 128), float(ZERO_AT), F32) for _ in range(4)]
        for j in range(96):
            w = jnp.broadcast_to(where[:, j : j + 1], (8, 128))
            v = jnp.broadcast_to(what[:, j : j + 1], (8, 128))
            for q in range(4):
                found[q] = jnp.where(w == lane_f + 128.0 * q, v, found[q])
        for q in range(4):
            packed[q, rows, :] = jnp.where(lane == 127, packed[q, rows, :], found[q].astype(jnp.int32))
        return carry

    lax.fori_loop(0, ROWS // 8, compact, 0)
    for k in range(1, 4):
        to = lax.rem(x + k, 4)
        remote(packed.at[to], lists.at[x], send_l.at[k], recv_l.at[x], space, to * 4 + four).start()
    keep_list = pltpu.make_async_copy(packed.at[x], lists.at[x], local_sem.at[4])
    keep_list.start()

    def hand_on(make, table, part):
        for k, (delta, flip) in enumerate(DIRECT):
            @guarded(delta)
            def _(k=k, delta=delta, flip=flip):
                slot = (1 + delta) * 4 + (four_y if flip else four)
                source = table.at[slot] if part is None else table.at[slot, part]
                make(source, slot, k, space, leaf).wait_recv()
                make(source, slot, 6 + k, space, sibling).start()

    hand_on(node_copy, node_tab, None)

    for k in range(1, n_space):
        source = lax.rem(space + k, n_space)
        remote(
            entry, two_tab.at[four * n_space + source], send_e.at[0], recv_e.at[source], space, leaf
        ).wait_recv()
    keep_two.wait()

    def band(which):
        return two_tab.at[pl.ds(which * n_space, n_space)]

    remote(band(four), band(four), send_b.at[0], recv_b.at[four], space, other_y).start()
    remote(band(four), band(four), send_b.at[1], recv_b.at[four], space, sibling).start()

    hand_on(leaf_copy, coef_tab, LEAF_PART)
    hand_on(one_copy, coef_tab, ONE_PART)

    remote(band(four_y), band(four_y), send_b.at[0], recv_b.at[four_y], space, other_y).wait_recv()
    remote(band(four_y), band(four_y), send_b.at[2], recv_b.at[four_y], space, sibling).start()

    beside = y_lo * 2 + (1 - core)
    beside_y = (1 - y_lo) * 2 + (1 - core)

    def last(make, table, part):
        for delta, flip in ((0, 0),) + DIRECT:
            @guarded(delta)
            def _(delta=delta, flip=flip):
                slot = (1 + delta) * 4 + (beside_y if flip else beside)
                source = table.at[slot] if part is None else table.at[slot, part]
                make(source, slot, 5, space, sibling).wait_recv()

    last(node_copy, node_tab, None)
    last(leaf_copy, coef_tab, LEAF_PART)
    last(one_copy, coef_tab, ONE_PART)
    for which in (beside, beside_y):
        remote(band(which), band(which), send_b.at[1], recv_b.at[which], space, sibling).wait_recv()
    for k in range(1, 4):
        source = lax.rem(x + k, 4)
        remote(nodes, target_nodes.at[source], send_x.at[k], recv_x.at[source], space, leaf).wait_recv()
        remote(packed.at[0], lists.at[source], send_l.at[k], recv_l.at[source], space, leaf).wait_recv()

    def sent(make, src, table, part):
        for k, (delta, flip) in enumerate(DIRECT):
            @guarded(delta)
            def _(k=k, delta=delta, flip=flip):
                make(src, (1 - delta) * 4 + four, k, *place(delta, flip)).wait_send()
                slot = (1 + delta) * 4 + (four_y if flip else four)
                source = table.at[slot] if part is None else table.at[slot, part]
                make(source, slot, 6 + k, space, sibling).wait_send()
        make(src, mine, 5, space, sibling).wait_send()

    sent(node_copy, nodes, node_tab, None)
    sent(leaf_copy, coef.at[LEAF_PART], coef_tab, LEAF_PART)
    sent(one_copy, coef.at[ONE_PART], coef_tab, ONE_PART)
    for k in range(1, n_space):
        two_copy(k).wait_send()
    remote(band(four), band(four), send_b.at[0], recv_b.at[four], space, other_y).wait_send()
    remote(band(four), band(four), send_b.at[1], recv_b.at[four], space, sibling).wait_send()
    remote(band(four_y), band(four_y), send_b.at[2], recv_b.at[four_y], space, sibling).wait_send()
    for k in range(1, 4):
        to = lax.rem(x + k, 4)
        remote(nodes, target_nodes.at[x], send_x.at[k], recv_x.at[x], space, to * 4 + four).wait_send()
        remote(packed.at[to], lists.at[x], send_l.at[k], recv_l.at[x], space, to * 4 + four).wait_send()
    for keep in keeps:
        keep.wait()
    keep_list.wait()


def upward(n_space, charges, basis, t_one, t_two, nodes, links):
    vmem = pl.BlockSpec(memory_space=pltpu.VMEM)
    hbm = pl.BlockSpec(memory_space=pl.ANY)
    dma = pltpu.SemaphoreType.DMA
    return pl.pallas_call(
        functools.partial(up_kernel, n_space),
        out_shape=(
            jax.ShapeDtypeStruct((12, 3 * PLANE, 128), BF16),
            jax.ShapeDtypeStruct((12, 36, 16, 128), BF16),
            jax.ShapeDtypeStruct((64, 16, 128), BF16),
            jax.ShapeDtypeStruct((4, 3 * PLANE, 128), BF16),
            jax.ShapeDtypeStruct((4, ROWS, 128), jnp.int32),
        ),
        in_specs=[vmem] * 6,
        out_specs=[hbm] * 5,
        scratch_shapes=[
            pltpu.VMEM((PAIRS, 16, 128), BF16),
            pltpu.VMEM((16, 128), BF16),
            pltpu.VMEM((4, ROWS, 128), jnp.int32),
            pltpu.VMEM((ROWS, 128), F32),
            pltpu.VMEM((ROWS, 128), F32),
            dma((5,)),
            dma((11,)), dma((11,)), dma((11,)),
            dma((12,)), dma((12,)), dma((12,)),
            dma((16,)), dma((16,)),
            dma((3,)), dma((4,)),
            dma((4,)), dma((4,)),
            dma((4,)), dma((4,)),
        ],
        compiler_params=pltpu.CompilerParams(
            collective_id=0, has_side_effects=True, vmem_limit_bytes=24 * 1024 * 1024
        ),
        name="upward",
    )(charges, basis, t_one, t_two, nodes, links)


def couple_kernel(
    lists, node_tab, coef_tab, two_tab, target_nodes, out, table, targets, total, feat
):
    def fill(planes, base, sources):
        px, py, pz = (planes[base, pl.ds(c * PLANE, PLANE), :].astype(F32) for c in range(3))
        norm = split3(px * px + py * py + pz * pz)
        ones = jnp.ones((PLANE, 128), F32)
        zeros = jnp.zeros((PLANE, 128), F32)
        if sources:
            parts = (px, py, pz) + norm + (ones,) * 3
        else:
            parts = (-2.0 * px, -2.0 * py, -2.0 * pz) + (ones,) * 3 + norm
        for k, part in enumerate(parts):
            feat[pl.ds(k, PLANE, stride=16), :] = part

    zeros = jnp.zeros((PLANE, 128), F32)
    for k in range(9, 16):
        feat[pl.ds(k, PLANE, stride=16), :] = zeros

    def one_source(slot, carry):
        fill(node_tab, slot, True)
        for i in range(36):
            f = feat[16 * i : 16 * i + 16, :].astype(BF16)
            c = coef_tab[slot, i]
            table[slot * SLOT + 2 * i] = jnp.concatenate([f[:, :RANK], c[:, :RANK]], axis=1)
            table[slot * SLOT + 2 * i + 1] = jnp.concatenate([f[:, RANK:], c[:, RANK:]], axis=1)
        return carry

    lax.fori_loop(0, 12, one_source, 0)
    table[pl.ds(TWO_AT, 64)] = two_tab[...]
    table[ZERO_AT] = jnp.zeros((16, 128), BF16)

    def one_target(slot, carry):
        fill(target_nodes, slot, False)
        for i in range(40):
            f = feat[16 * i : 16 * i + 16, :]
            start = pl.multiple_of(slot * (ROWS * RANK) + i * 128, 128)
            targets[pl.ds(start, 128), :] = f.T.astype(BF16)
        return carry

    lax.fori_loop(0, 4, one_target, 0)

    def clear(i, carry):
        for j in range(16):
            total[i * 16 + j] = jnp.zeros((16, RANK), F32)
        return carry

    lax.fori_loop(0, 4 * ROWS // 16, clear, 0)

    end = 4 * ROWS - 1

    def step(carry):
        r, t, g = carry
        for _ in range(UNROLL):
            picked = [table[lists[r, 4 * g + i]] for i in range(4)]
            sources = jnp.concatenate([e[:, :RANK] for e in picked], axis=1)
            coefs = jnp.concatenate([e[:, RANK:] for e in picked], axis=1)
            mine = targets[pl.ds(pl.multiple_of(r * RANK, RANK), RANK), :]
            square = jnp.maximum(jnp.dot(mine, sources, preferred_element_type=F32), 1e-20)
            dist = square * lax.rsqrt(square)
            matrix = ((dist + 1.0 / SCALE) * jnp.exp2(dist * (-SCALE * LOG2E))).astype(BF16)
            total[r] += nt(coefs, matrix)
            done = g + 1 >= lists[r, 127]
            over = t == 72
            r = jnp.where(done, jnp.minimum(jnp.where(over, r + 8, r + 1), end), r)
            t = jnp.where(done, jnp.where(over, 0, t + 1), t)
            g = jnp.where(done, 0, g + 1)
        return r, t, g

    lax.while_loop(lambda c: c[0] < end, step, (jnp.int32(0), jnp.int32(0), jnp.int32(0)))

    def pack(i, carry):
        for q in range(4):
            at = q * ROWS + 2 * i
            both = jnp.concatenate([total[at], total[at + 1]], axis=1)
            out[q, i] = (both * (AMPLITUDE * SCALE)).astype(BF16)
        return carry

    lax.fori_loop(0, PAIRS, pack, 0)


def coupling(lists, node_tab, coef_tab, two_tab, target_nodes):
    vmem = pl.BlockSpec(memory_space=pltpu.VMEM)
    return pl.pallas_call(
        couple_kernel,
        grid_spec=pltpu.PrefetchScalarGridSpec(
            num_scalar_prefetch=1,
            grid=(),
            in_specs=[vmem] * 4,
            out_specs=vmem,
            scratch_shapes=[
                pltpu.VMEM((ENTRIES, 16, 128), BF16),
                pltpu.VMEM((4 * ROWS * RANK, 16), BF16),
                pltpu.VMEM((4 * ROWS, 16, RANK), F32),
                pltpu.VMEM((PLANE * 16, 128), F32),
            ],
        ),
        out_shape=jax.ShapeDtypeStruct((4, PAIRS, 16, 128), BF16),
        compiler_params=pltpu.CompilerParams(vmem_limit_bytes=40 * 1024 * 1024),
        name="coupling",
    )(lists, node_tab, coef_tab, two_tab, target_nodes)


def down_kernel(far, basis, t_one, t_two, out, came, near, send, recv):
    space = lax.axis_index("space")
    leaf = lax.axis_index("leaf")
    x = leaf // 4
    four = lax.rem(leaf, 4)
    barrier = pltpu.get_barrier_semaphore()
    for k in range(1, 4):
        to = lax.rem(x + k, 4) * 4 + four
        pl.semaphore_signal(barrier, inc=1, device_id=(space, to), device_id_type=MESH)
    pl.semaphore_wait(barrier, 3)

    def copy(k):
        to = lax.rem(x + k, 4)
        return pltpu.make_async_remote_copy(
            src_ref=far.at[to], dst_ref=came.at[x], send_sem=send.at[k], recv_sem=recv.at[x],
            device_id=(space, to * 4 + four), device_id_type=MESH,
        )

    for k in range(1, 4):
        copy(k).start()
    came[x] = far[x]
    for k in range(1, 4):
        source = lax.rem(x + k, 4)
        pltpu.make_async_remote_copy(
            src_ref=far.at[source], dst_ref=came.at[source], send_sem=send.at[k], recv_sem=recv.at[source],
            device_id=(space, leaf), device_id_type=MESH,
        ).wait_recv()

    def summed(i):
        return (
            came[0, i].astype(F32) + came[1, i].astype(F32)
            + came[2, i].astype(F32) + came[3, i].astype(F32)
        )

    local_two = summed(36)[:, :RANK].astype(BF16)
    down_one = jnp.dot(local_two, t_two[0], preferred_element_type=F32)
    for i in range(4):
        near[32 + i] = (summed(32 + i) + down_one[:, 128 * i : 128 * i + 128]).astype(BF16)

    def cluster(i, carry):
        both = near[32 + i]
        for h in range(2):
            local_one = both[:, h * RANK : (h + 1) * RANK]
            down_leaf = jnp.dot(local_one, t_one[2 * i + h], preferred_element_type=F32)
            for j in range(4):
                pair = 8 * i + 4 * h + j
                local_leaf = (summed(pair) + down_leaf[:, 128 * j : 128 * j + 128]).astype(BF16)
                for s in range(2):
                    at = pl.multiple_of((2 * pair + s) * 128, 128)
                    out[:, pl.ds(at, 128)] = jnp.dot(
                        local_leaf[:, s * RANK : (s + 1) * RANK], basis[2 * pair + s],
                        preferred_element_type=F32,
                    ).astype(BF16)
        return carry

    lax.fori_loop(0, 4, cluster, 0)
    for k in range(1, 4):
        copy(k).wait_send()


def downward(far, basis, t_one, t_two):
    vmem = pl.BlockSpec(memory_space=pltpu.VMEM)
    dma = pltpu.SemaphoreType.DMA
    return pl.pallas_call(
        down_kernel,
        out_shape=jax.ShapeDtypeStruct((16, LEAF_DEV * 128), BF16),
        in_specs=[vmem] * 4,
        out_specs=vmem,
        scratch_shapes=[
            pltpu.VMEM((4, PAIRS, 16, 128), BF16),
            pltpu.VMEM((36, 16, 128), BF16),
            dma((4,)), dma((4,)),
        ],
        compiler_params=pltpu.CompilerParams(
            collective_id=1, has_side_effects=True, vmem_limit_bytes=24 * 1024 * 1024
        ),
        name="downward",
    )(far, basis, t_one, t_two)


def packed_nodes(*levels):
    rows = []
    for nodes in levels:
        flat = nodes.transpose(1, 0, 2).reshape(3, -1)
        flat = jnp.pad(flat, ((0, 0), (0, -flat.shape[1] % 128)))
        rows.append(flat.reshape(3, -1, 128))
    whole = jnp.concatenate(rows, axis=1)
    whole = jnp.pad(whole, ((0, 0), (0, PLANE - whole.shape[1]), (0, 0)))
    return whole.reshape(3 * PLANE, 128)


def coded_links(links_leaf, links_one, links_two, space):
    def near(links, per_dev, offset):
        owner = links // per_dev
        slot = (owner // 16 - space + 1) * 4 + owner % 4
        return owner // 4 % 4 * 1024 + slot * SLOT + offset + links % per_dev

    two = links_two // 4 % 4 * 1024 + TWO_AT + links_two % 4 * 16 + links_two // 16
    links = jnp.concatenate([links_leaf, links_one, links_two], axis=0)
    codes = jnp.concatenate(
        [near(links_leaf, LEAF_DEV, 0), near(links_one, ONE_DEV, LEAF_DEV), two], axis=0
    )
    codes = jnp.where(links >= 0, codes, 4096)
    rows, slots = codes.shape
    return jnp.pad(codes, ((0, ROWS - rows), (0, 128 - slots)), constant_values=4096)


def local(
    charges, leaf_basis, transfer_one, transfer_two, nodes_leaf, nodes_one, nodes_two,
    links_leaf, links_one, links_two,
):
    n_space = lax.axis_size("space")
    nodes = packed_nodes(nodes_leaf, nodes_one, nodes_two)
    links = coded_links(links_leaf, links_one, links_two, lax.axis_index("space"))
    node_tab, coef_tab, two_tab, target_nodes, lists = upward(
        n_space, charges, leaf_basis, transfer_one, transfer_two, nodes, links
    )
    far = coupling(lists.reshape(4 * ROWS, 128), node_tab, coef_tab, two_tab, target_nodes)
    return downward(far, leaf_basis, transfer_one, transfer_two)


def solution(mesh):
    return jax.shard_map(
        local,
        mesh=mesh,
        in_specs=(
            P(None, ("space", "leaf")),
            P(("space", "leaf"), None, None),
            P(("space", "leaf"), None, None),
            P(("space", "leaf"), None, None),
            P(("space", "leaf"), None, None),
            P(("space", "leaf"), None, None),
            P(("space", "leaf"), None, None),
            P(("space", "leaf"), None),
            P(("space", "leaf"), None),
            P(("space", "leaf"), None),
        ),
        out_specs=P(None, ("space", "leaf")),
        check_vma=False,
    )
```

time: 1380 us -> 111 us (0.08)
  the two profiles are of different devices: /device:TPU:137 before, /device:TPU:32 now
where the time goes in v1:
time: 111 us; the launch traced here: 110 us
  Pallas kernels  100 us (90%)
  local copies, waits for them, and re-layouts  7.14 us (6%)
  other arithmetic  3.07 us (3%)
    pallas_call x1, Pallas kernels, coupling(): pl.pallas_call(couple_kernel, grid_spec=pltpu.PrefetchScalarGridSpec(num_...  57 us
    pallas_call x1, Pallas kernels, upward(): pl.pallas_call(functools.partial(up_kernel, n_space), out_shape=(jax.Shap...  30.5 us
    pallas_call x1, Pallas kernels, downward(): pl.pallas_call(down_kernel, out_shape=jax.ShapeDtypeStruct((16, LEAF_DEV...  12.5 us
    unnamed x15, local copies, waits for them, and re-layouts  4.77 us
    reshape x4, local copies, waits for them, and re-layouts, packed_nodes(): rows.append(flat.reshape(3, -1, 128))  2.36 us

profile of v1, /device:TPU:32, one launch (start us, length us, event | category | flops | bytes accessed | tf_op | source)
XLA Modules:
  0.0 110.3 jit_solution(11686625269579184719)
XLA Ops:
  0.0 0.7 fusion.39
  0.7 0.7 pad_bitcast_fusion
  1.4 0.8 reshape.20
  2.1 0.7 fusion.24
  2.9 0.9 reshape.19
  3.8 0.9 fusion.8
  4.6 0.8 add_select_fusion.6
  5.5 0.0 copy-start
  5.5 1.2 %copy-done = bf16[64,64,128]{2,1,0:T(8,128)(2,1)S(1)} copy-done((bf16[64,64,128]{2,1,0:T(8,128)(2,1)S(1)}, bf16[64,64,128]{2,1,0:T(8,128)(2,1)}, u32[]{:S(2)}) %copy-start) | copy-done | bytes 1048600
  6.7 0.0 copy-start.2
  6.7 1.0 copy-done.2
  7.7 0.0 copy-start.4
  7.7 0.9 copy-done.4
  8.7 0.0 copy-start.5
  8.7 0.8 copy-done.5
  9.5 30.5 %upward.1 = (bf16[12,144,128]{2,1,0:T(8,128)(2,1)S(1)}, bf16[12,36,16,128]{3,2,1,0:T(8,128)(2,1)S(1)}, bf16[64,16,128]{2,1,0:T(8,128)(2,1)S(1)}, bf16[4,144,128]{2,1,0:T(8,128)(2,1)S(1)}, s32[4,80,128]{2,1,0:T(8,128)S(1)}) custom-call(bf16[16,8192]{1,0:T(8,128)(2,1)S(1)} %copy-done.4, bf16[64,64,128]{2,1,0:T(8,128)(2,1)S(1)} %copy-done, ...), custom_call_target="tpu_custom_call" | custom-call | tf_op jit(solution)/shard_map/upward/pallas_call | solution.py:300
  40.1 0.0 copy-start.1
  40.1 0.0 copy-start.3
  40.1 0.0 copy-start.6
  40.1 57.0 %coupling.1.far = bf16[4,37,16,128]{3,2,1,0:T(8,128)(2,1)S(1)} custom-call(s32[320,128]{1,0:T(8,128)S(1)} %bitcast.7, bf16[12,144,128]{2,1,0:T(8,128)(2,1)S(1)} %get-tuple-element.11.node_tab, bf16[12,36,16,128]{3,2,1,0:T(8,128)(2,1)S(1)} %get-tuple-element.12.coef_tab, bf16[64,16,128]{2,1,0:T(8,128)(2,1)S(1)} %get-tuple-element.13.two_tab, ...), custom_call_target="tpu_custom_call" | custom-call | tf_op jit(solution)/shard_map/coupling/pallas_call | solution.py:415
  97.1 0.0 copy-done.1
  97.1 0.0 copy-done.3
  97.2 0.0 copy-done.6
  97.2 12.5 %downward.1 = bf16[16,8192]{1,0:T(8,128)(2,1)S(1)} custom-call(bf16[4,37,16,128]{3,2,1,0:T(8,128)(2,1)S(1)} %coupling.1.far, bf16[64,64,128]{2,1,0:T(8,128)(2,1)S(1)} %copy-done.1, bf16[8,64,512]{2,1,0:T(8,128)(2,1)S(1)} %copy-done.3, bf16[1,64,512]{2,1,0:T(8,128)(2,1)S(1)} %copy-done.6), custom_call_target="tpu_custom_call" | custom-call | tf_op jit(solution)/shard_map/downward/pallas_call | solution.py:498
  109.6 0.7 copy.13
  (3 shorter events, 0.0 us)
Async XLA Ops:
  5.5 1.2 %copy-start = (bf16[64,64,128]{2,1,0:T(8,128)(2,1)S(1)}, bf16[64,64,128]{2,1,0:T(8,128)(2,1)}, u32[]{:S(2)}) copy-start(bf16[64,64,128]{2,1,0:T(8,128)(2,1)} %basis.3) | copy-start | bytes 3145732
  6.7 1.0 copy-start.2
  7.7 0.9 copy-start.4
  8.7 0.8 copy-start.5
  40.1 57.1 %copy-start.1 = (bf16[64,64,128]{2,1,0:T(8,128)(2,1)S(1)}, bf16[64,64,128]{2,1,0:T(8,128)(2,1)}, u32[]{:S(2)}) copy-start(bf16[64,64,128]{2,1,0:T(8,128)(2,1)} %basis.3) | copy-start | bytes 3145732
  40.1 57.1 %copy-start.3 = (bf16[8,64,512]{2,1,0:T(8,128)(2,1)S(1)}, bf16[8,64,512]{2,1,0:T(8,128)(2,1)}, u32[]{:S(2)}) copy-start(bf16[8,64,512]{2,1,0:T(8,128)(2,1)} %t_one.3) | copy-start | bytes 1572868
  40.1 57.1 %copy-start.6 = (bf16[1,64,512]{2,1,0:T(8,128)(2,1)S(1)}, bf16[1,64,512]{2,1,0:T(8,128)(2,1)}, u32[]{:S(2)}) copy-start(bf16[1,64,512]{2,1,0:T(8,128)(2,1)} %t_two.3) | copy-start | bytes 196612

commit v2 on v1

v2 whole, which is shorter than its diff:
```python
import functools

import jax
import jax.numpy as jnp
from jax import lax
from jax.experimental import pallas as pl
from jax.experimental.pallas import tpu as pltpu
from jax.sharding import PartitionSpec as P

SCALE = 1.7320508075688772 / 2.0
AMPLITUDE = 0.25
LOG2E = 1.4426950408889634
MESH = pl.DeviceIdType.MESH
F32 = jnp.float32
BF16 = jnp.bfloat16

RANK = 64
LEAF_DEV = 64
ONE_DEV = 8
PAIRS = 37
PLANE = 48
ROWS = 80
SLOT = 72
TWO_AT = 12 * SLOT
ZERO_AT = TWO_AT + 64
ENTRIES = ZERO_AT + 8
UNROLL = 96

PIECES = 3
CUT = 16
BLOCKS = 5
VMEM_BYTES = 58 * 1024 * 1024


def nt(a, b):
    return lax.dot_general(a, b, (((1,), (1,)), ((), ())), preferred_element_type=F32)


def split3(value):
    first = value.astype(BF16).astype(F32)
    rest = value - first
    second = rest.astype(BF16).astype(F32)
    return first, second, rest - second


def up_kernel(
    n_space,
    charges_in, basis_in, t_one_in, t_two_in, leaf_nodes_in, one_nodes_in, two_nodes_in,
    leaf_links_in, one_links_in, two_links_in,
    table_out, blocks_out, lists,
    charges, basis, t_one, t_two, leaf_nodes, one_nodes, two_nodes, leaf_links, one_links, two_links,
    nodes_f, nodes, coef, entry, packed, order, value, feat, feat_t,
    node_tab, coef_tab, two_tab, target_nodes, table, blocks,
    in_sem, out_sem, local_sem, send_own, send_relay, send_z, send_sib, recv,
    send_e, recv_e, send_b, recv_b, send_x, recv_x, send_l, recv_l,
):
    space = lax.axis_index("space")
    leaf = lax.axis_index("leaf")
    x = leaf // 4
    four = lax.rem(leaf, 4)
    y_lo = four // 2
    core = lax.rem(four, 2)
    four_y = (1 - y_lo) * 2 + core
    beside = y_lo * 2 + (1 - core)
    beside_y = (1 - y_lo) * 2 + (1 - core)
    other_y = x * 4 + four_y
    sibling = x * 4 + beside
    side = 1 - 2 * lax.rem(space, 2)
    plane = space + side
    ahead = space + 2 * side
    behind = space - 2 * side
    has_ahead = (ahead >= 0) & (ahead < n_space)
    has_behind = (behind >= 0) & (behind < n_space)
    near, far = (1 + side) * 4, (1 - side) * 4

    loads = [
        pltpu.make_async_copy(src, dst, in_sem.at[k])
        for k, (src, dst) in enumerate(
            (
                (leaf_nodes_in, leaf_nodes), (one_nodes_in, one_nodes), (two_nodes_in, two_nodes),
                (charges_in, charges), (basis_in, basis), (t_one_in, t_one), (t_two_in, t_two),
                (leaf_links_in, leaf_links), (one_links_in, one_links), (two_links_in, two_links),
            )
        )
    ]
    for load in loads:
        load.start()

    barrier = pltpu.get_barrier_semaphore()

    def greet(s, l):
        pl.semaphore_signal(barrier, inc=1, device_id=(s, l), device_id_type=MESH)

    for k in range(1, 4):
        greet(space, lax.rem(x + k, 4) * 4 + four)
    for k in range(1, n_space):
        greet(lax.rem(space + k, n_space), leaf)
    greet(space, other_y)
    greet(plane, other_y)
    greet(space, sibling)

    nodes_f[...] = jnp.zeros((3 * PLANE, 128), F32)
    for load in loads[:3]:
        load.wait()
    for c in range(3):
        base = c * PLANE
        value[0:64, 0:RANK] = leaf_nodes[c].astype(F32)
        value[64:72, 0:RANK] = one_nodes[c].astype(F32)
        for h in range(2):
            nodes_f[base : base + 36, h * RANK : (h + 1) * RANK] = value[pl.ds(h, 36, stride=2), 0:RANK]
        nodes_f[base + 36 : base + 37, 0:RANK] = two_nodes[c : c + 1].astype(F32)
    nodes[...] = nodes_f[...].astype(BF16)

    def remote(src, dst, send, came, s, l):
        return pltpu.make_async_remote_copy(
            src_ref=src, dst_ref=dst, send_sem=send, recv_sem=came, device_id=(s, l), device_id_type=MESH
        )

    mine = 4 + four
    parts = (None, pl.ds(0, CUT), pl.ds(CUT, 36 - CUT))

    def own(piece):
        return nodes if piece == 0 else coef.at[parts[piece]]

    def held(piece, slot):
        return node_tab.at[slot] if piece == 0 else coef_tab.at[slot, parts[piece]]

    def move(piece, src, slot, send, s, l):
        return remote(src, held(piece, slot), send, recv.at[piece, slot], s, l)

    def own_copies(piece):
        return (
            move(piece, own(piece), 4 + four, send_own.at[piece, 0], space, other_y),
            move(piece, own(piece), far + four, send_own.at[piece, 1], plane, other_y),
            move(piece, own(piece), mine, send_own.at[piece, 2], space, sibling),
        )

    def send_all(piece):
        for copy in own_copies(piece):
            copy.start()

    slot_a, slot_b, slot_c = 4 + four_y, near + four_y, near + four
    slot_z = (far + four_y, far + four)

    def arrived(piece, slot):
        move(piece, held(piece, slot), slot, send_own.at[piece, 0], space, sibling).wait_recv()

    def relay_copy(piece):
        return (
            move(piece, held(piece, slot_a), far + four_y, send_relay.at[piece], plane, other_y),
            move(piece, held(piece, slot_b), near + four_y, send_relay.at[piece], space, other_y),
        )

    def z_copy(piece, which):
        slot = (slot_b, slot_c)[which]
        return move(piece, held(piece, slot), slot_z[which], send_z.at[piece, which], ahead, leaf)

    def sib_copy(piece, which):
        slot = (slot_a, slot_b, slot_c) + slot_z
        return move(piece, held(piece, slot[which]), slot[which], send_sib.at[piece, which], space, sibling)

    def pass_ab(piece):
        by_a, by_b = relay_copy(piece)
        arrived(piece, slot_a)

        @pl.when(core == 0)
        def _():
            by_a.start()

        sib_copy(piece, 0).start()
        arrived(piece, slot_b)

        @pl.when(core == 1)
        def _():
            by_b.start()

        @pl.when(has_ahead)
        def _():
            z_copy(piece, 0).start()

        sib_copy(piece, 1).start()

    def pass_c(piece):
        arrived(piece, slot_c)

        @pl.when(has_ahead)
        def _():
            z_copy(piece, 1).start()

        sib_copy(piece, 2).start()

    def pass_z(piece):
        @pl.when(has_behind)
        def _():
            for which in range(2):
                arrived(piece, slot_z[which])
                sib_copy(piece, 3 + which).start()

    def leaves(i, carry):
        for j in range(4):
            pair = i * 4 + j
            halves = [
                nt(charges[:, pl.ds(pl.multiple_of((2 * pair + h) * 128, 128), 128)], basis[2 * pair + h])
                for h in range(2)
            ]
            coef[pair] = jnp.concatenate(halves, axis=1).astype(BF16)
        return carry

    pl.semaphore_wait(barrier, 3 + (n_space - 1) + 3)
    send_all(0)
    for k in range(1, 4):
        to = lax.rem(x + k, 4) * 4 + four
        remote(nodes, target_nodes.at[x], send_x.at[k], recv_x.at[x], space, to).start()
    loads[3].wait()
    loads[4].wait()
    lax.fori_loop(0, CUT // 4, leaves, 0)
    send_all(1)
    lax.fori_loop(CUT // 4, 8, leaves, 0)

    loads[5].wait()
    for i in range(4):
        halves = []
        for h in range(2):
            p = 2 * i + h
            stacked = jnp.concatenate([coef[4 * p + j] for j in range(4)], axis=1)
            halves.append(nt(stacked, t_one[p]))
        coef[32 + i] = jnp.concatenate(halves, axis=1).astype(BF16)
    send_all(2)
    pass_ab(0)

    loads[6].wait()
    top = nt(jnp.concatenate([coef[32 + j] for j in range(4)], axis=1), t_two[0])
    tx, ty, tz = (nodes_f[c * PLANE + 36 : c * PLANE + 37, 0:RANK] for c in range(3))
    rows = (tx, ty, tz) + split3(tx * tx + ty * ty + tz * tz)
    row = lax.broadcasted_iota(jnp.int32, (16, RANK), 0)
    feature = jnp.where((row >= 6) & (row < 9), 1.0, 0.0)
    for k, part in enumerate(rows):
        feature = jnp.where(row == k, jnp.broadcast_to(part, (16, RANK)), feature)
    entry[...] = jnp.concatenate([feature, top], axis=1).astype(BF16)

    own_two = four * n_space + space

    def two_copy(k):
        return remote(
            entry, two_tab.at[own_two], send_e.at[k], recv_e.at[space],
            lax.rem(space + k, n_space), leaf,
        )

    for k in range(1, n_space):
        two_copy(k).start()
    two_tab[own_two] = entry[...]

    for load in loads[7:]:
        load.wait()

    def code(links, per_dev, offset):
        owner = links // per_dev
        slot = (owner // 16 - space + 1) * 4 + owner % 4
        coded = owner // 4 % 4 * 1024 + slot * SLOT + offset + links % per_dev
        return jnp.where(links >= 0, coded, 4096)

    packed[0] = jnp.full((ROWS, 128), 4096, jnp.int32)
    packed[0, 0:64, 0:96] = code(leaf_links[...], LEAF_DEV, 0)
    packed[0, 64:72, 0:96] = code(one_links[...], ONE_DEV, LEAF_DEV)
    two = two_links[...]
    packed[0, 72:73, 0:96] = jnp.where(
        two >= 0, two // 4 % 4 * 1024 + TWO_AT + two % 4 * 16 + two // 16, 4096
    )
    codes = packed[0]
    group = codes // 1024
    before = jnp.where(
        lax.broadcasted_iota(jnp.int32, (128, 128), 0) < lax.broadcasted_iota(jnp.int32, (128, 128), 1), 1.0, 0.0
    ).astype(BF16)
    at = jnp.full((ROWS, 128), -1.0, F32)
    counts = []
    for q in range(4):
        member = jnp.where(group == q, 1.0, 0.0)
        rank = jnp.dot(member.astype(BF16), before, preferred_element_type=F32)
        at = jnp.where(group == q, rank + 128.0 * q, at)
        counts.append(jnp.sum(member, axis=1, keepdims=True))
    order[...] = at
    value[...] = (codes - group * 1024).astype(F32)
    lane = lax.broadcasted_iota(jnp.int32, (8, 128), 1)
    lane_f = lane.astype(F32)
    for q in range(4):
        packed[q] = jnp.broadcast_to(jnp.maximum((counts[q].astype(jnp.int32) + 3) // 4, 1), (ROWS, 128))
    pass_ab(1)

    def compact(b, carry):
        block = pl.ds(pl.multiple_of(b * 8, 8), 8)
        where = order[block, :]
        what = value[block, :]
        found = [jnp.full((8, 128), float(ZERO_AT), F32) for _ in range(4)]
        for j in range(96):
            w = jnp.broadcast_to(where[:, j : j + 1], (8, 128))
            v = jnp.broadcast_to(what[:, j : j + 1], (8, 128))
            for q in range(4):
                found[q] = jnp.where(w == lane_f + 128.0 * q, v, found[q])
        for q in range(4):
            packed[q, block, :] = jnp.where(lane == 127, packed[q, block, :], found[q].astype(jnp.int32))
        return carry

    lax.fori_loop(0, ROWS // 8, compact, 0)
    for k in range(1, 4):
        to = lax.rem(x + k, 4)
        remote(packed.at[to], lists.at[x], send_l.at[k], recv_l.at[x], space, to * 4 + four).start()
    keep_list = pltpu.make_async_copy(packed.at[x], lists.at[x], local_sem)
    keep_list.start()
    pass_c(0)
    pass_ab(2)
    pass_c(1)
    pass_z(0)

    def planes(source):
        px, py, pz = (source[c * PLANE : (c + 1) * PLANE, :].astype(F32) for c in range(3))
        return px, py, pz, split3(px * px + py * py + pz * pz)

    ones = jnp.ones((PLANE, 128), F32)
    zeros = jnp.zeros((PLANE, 128), F32)
    for k in range(6, 16):
        feat[pl.ds(k, PLANE, stride=16), :] = ones if k < 9 else zeros
    for k in range(3, 16):
        feat_t[pl.ds(k, PLANE, stride=16), :] = ones if k < 6 else zeros

    def table_copy(slot):
        part = pl.ds(slot * SLOT, SLOT)
        return pltpu.make_async_copy(table.at[part], table_out.at[part], out_sem.at[slot])

    def enter(slot, source, coefs):
        px, py, pz, norm = planes(source)
        for k, part in enumerate((px, py, pz) + norm):
            feat[pl.ds(k, PLANE, stride=16), :] = part

        def some(b, carry):
            for j in range(6):
                i = b * 6 + j
                f = feat[pl.ds(pl.multiple_of(i * 16, 16), 16), :].astype(BF16)
                c = coefs(i)
                table[slot * SLOT + 2 * i] = jnp.concatenate([f[:, :RANK], c[:, :RANK]], axis=1)
                table[slot * SLOT + 2 * i + 1] = jnp.concatenate([f[:, RANK:], c[:, RANK:]], axis=1)
            return carry

        lax.fori_loop(0, 6, some, 0)
        table_copy(slot).start()

    def enter_held(slot):
        enter(slot, node_tab.at[slot], lambda i: coef_tab[slot, i])

    def aim(which, source):
        px, py, pz, norm = planes(source)
        for k, part in enumerate((-2.0 * px, -2.0 * py, -2.0 * pz)):
            feat_t[pl.ds(k, PLANE, stride=16), :] = part
        for k, part in enumerate(norm):
            feat_t[pl.ds(6 + k, PLANE, stride=16), :] = part

        for b in range(BLOCKS):
            blocks[which * BLOCKS + b] = feat_t[b * 128 : (b + 1) * 128, :].T.astype(BF16)

    aim(x, nodes)
    pass_c(2)
    pass_z(1)
    enter(mine, nodes, lambda i: coef[i])
    table[pl.ds(ZERO_AT, 8)] = jnp.zeros((8, 16, 128), BF16)
    pass_z(2)

    for k in range(1, n_space):
        source = lax.rem(space + k, n_space)
        remote(
            entry, two_tab.at[four * n_space + source], send_e.at[0], recv_e.at[source], space, leaf
        ).wait_recv()

    def band(which):
        return two_tab.at[pl.ds(which * n_space, n_space)]

    def band_copy(k):
        which, to = ((four, other_y), (four, sibling), (four_y, sibling))[k]
        return remote(band(which), band(which), send_b.at[k], recv_b.at[which], space, to)

    def band_arrived(which):
        remote(band(which), band(which), send_b.at[0], recv_b.at[which], space, sibling).wait_recv()

    band_copy(0).start()
    band_copy(1).start()

    for k in range(1, 4):
        source = lax.rem(x + k, 4)
        remote(nodes, target_nodes.at[source], send_x.at[k], recv_x.at[source], space, leaf).wait_recv()
        aim(source, target_nodes.at[source])

    band_arrived(four_y)
    band_copy(2).start()

    for slot in (slot_a, slot_b, slot_c):
        enter_held(slot)

    def from_sibling(slot):
        for piece in range(PIECES):
            arrived(piece, slot)
        enter_held(slot)

    for slot in (4 + beside, 4 + beside_y, near + beside_y, near + beside):
        from_sibling(slot)

    @pl.when(has_behind)
    def _():
        for slot in slot_z:
            enter_held(slot)
        for slot in (far + beside_y, far + beside):
            from_sibling(slot)

    band_arrived(beside)
    band_arrived(beside_y)
    table[pl.ds(TWO_AT, 64)] = two_tab[...]
    rest = pl.ds(TWO_AT, ENTRIES - TWO_AT)
    ends = (
        pltpu.make_async_copy(table.at[rest], table_out.at[rest], out_sem.at[12]),
        pltpu.make_async_copy(blocks, blocks_out, out_sem.at[13]),
    )
    for copy in ends:
        copy.start()
    for k in range(1, 4):
        source = lax.rem(x + k, 4)
        remote(packed.at[0], lists.at[source], send_l.at[k], recv_l.at[source], space, leaf).wait_recv()

    for piece in range(PIECES):
        for copy in own_copies(piece):
            copy.wait_send()
        relay_copy(piece)[0].wait_send()
        for which in range(3):
            sib_copy(piece, which).wait_send()

        @pl.when(has_ahead)
        def _(piece=piece):
            for which in range(2):
                z_copy(piece, which).wait_send()

        @pl.when(has_behind)
        def _(piece=piece):
            for which in range(2):
                sib_copy(piece, 3 + which).wait_send()

    for k in range(1, n_space):
        two_copy(k).wait_send()
    for k in range(3):
        band_copy(k).wait_send()
    for k in range(1, 4):
        to = lax.rem(x + k, 4)
        remote(nodes, target_nodes.at[x], send_x.at[k], recv_x.at[x], space, to * 4 + four).wait_send()
        remote(packed.at[to], lists.at[x], send_l.at[k], recv_l.at[x], space, to * 4 + four).wait_send()
    keep_list.wait()
    for slot in (mine, slot_a, slot_b, slot_c, 4 + beside, 4 + beside_y, near + beside_y, near + beside):
        table_copy(slot).wait()

    @pl.when(has_behind)
    def _():
        for slot in slot_z + (far + beside_y, far + beside):
            table_copy(slot).wait()

    for copy in ends:
        copy.wait()


def upward(n_space, *arrays):
    hbm = pl.BlockSpec(memory_space=pltpu.HBM)
    dma = pltpu.SemaphoreType.DMA
    return pl.pallas_call(
        functools.partial(up_kernel, n_space),
        out_shape=(
            jax.ShapeDtypeStruct((ENTRIES, 16, 128), BF16),
            jax.ShapeDtypeStruct((4 * BLOCKS, 128, 128), BF16),
            jax.ShapeDtypeStruct((4, ROWS, 128), jnp.int32),
        ),
        in_specs=[hbm] * len(arrays),
        out_specs=[hbm] * 3,
        scratch_shapes=[pltpu.VMEM(a.shape, a.dtype) for a in arrays]
        + [
            pltpu.VMEM((3 * PLANE, 128), F32),
            pltpu.VMEM((3 * PLANE, 128), BF16),
            pltpu.VMEM((PAIRS, 16, 128), BF16),
            pltpu.VMEM((16, 128), BF16),
            pltpu.VMEM((4, ROWS, 128), jnp.int32),
            pltpu.VMEM((ROWS, 128), F32),
            pltpu.VMEM((ROWS, 128), F32),
            pltpu.VMEM((PLANE * 16, 128), F32),
            pltpu.VMEM((PLANE * 16, 128), F32),
            pltpu.VMEM((12, 3 * PLANE, 128), BF16),
            pltpu.VMEM((12, 36, 16, 128), BF16),
            pltpu.VMEM((64, 16, 128), BF16),
            pltpu.VMEM((4, 3 * PLANE, 128), BF16),
            pltpu.VMEM((ENTRIES, 16, 128), BF16),
            pltpu.VMEM((4 * BLOCKS, 128, 128), BF16),
            dma((len(arrays),)), dma((14,)),
            dma,
            dma((PIECES, 3)), dma((PIECES,)), dma((PIECES, 2)), dma((PIECES, 5)), dma((PIECES, 12)),
            dma((16,)), dma((16,)),
            dma((3,)), dma((4,)),
            dma((4,)), dma((4,)),
            dma((4,)), dma((4,)),
        ],
        compiler_params=pltpu.CompilerParams(
            collective_id=0, has_side_effects=True, vmem_limit_bytes=VMEM_BYTES
        ),
        name="upward",
    )(*arrays)


def couple_kernel(lists, table_in, blocks_in, out, table, blocks, targets, total, sem):
    loads = (
        pltpu.make_async_copy(blocks_in, blocks, sem.at[0]),
        pltpu.make_async_copy(table_in, table, sem.at[1]),
    )
    for load in loads:
        load.start()

    def clear(i, carry):
        for j in range(16):
            total[i * 16 + j] = jnp.zeros((16, RANK), F32)
        return carry

    lax.fori_loop(0, 4 * ROWS // 16, clear, 0)
    loads[0].wait()

    def spread(b, carry):
        block = blocks[b]
        for j in range(8):
            start = pl.multiple_of((b * 8 + j) * 128, 128)
            targets[pl.ds(start, 128), :] = block[:, 16 * j : 16 * j + 16]
        return carry

    lax.fori_loop(0, 4 * BLOCKS, spread, 0)
    loads[1].wait()

    end = 4 * ROWS - 1

    def step(carry):
        r, t, g = carry
        for _ in range(UNROLL):
            picked = [table[lists[r, 4 * g + i]] for i in range(4)]
            sources = jnp.concatenate([e[:, :RANK] for e in picked], axis=1)
            coefs = jnp.concatenate([e[:, RANK:] for e in picked], axis=1)
            mine = targets[pl.ds(pl.multiple_of(r * RANK, RANK), RANK), :]
            square = jnp.maximum(jnp.dot(mine, sources, preferred_element_type=F32), 1e-20)
            dist = square * lax.rsqrt(square)
            matrix = ((dist + 1.0 / SCALE) * jnp.exp2(dist * (-SCALE * LOG2E))).astype(BF16)
            total[r] += nt(coefs, matrix)
            done = g + 1 >= lists[r, 127]
            over = t == 72
            r = jnp.where(done, jnp.minimum(jnp.where(over, r + 8, r + 1), end), r)
            t = jnp.where(done, jnp.where(over, 0, t + 1), t)
            g = jnp.where(done, 0, g + 1)
        return r, t, g

    lax.while_loop(lambda c: c[0] < end, step, (jnp.int32(0), jnp.int32(0), jnp.int32(0)))

    def pack(i, carry):
        for q in range(4):
            at = q * ROWS + 2 * i
            both = jnp.concatenate([total[at], total[at + 1]], axis=1)
            out[q, i] = (both * (AMPLITUDE * SCALE)).astype(BF16)
        return carry

    lax.fori_loop(0, PAIRS, pack, 0)


def coupling(lists, table, blocks):
    hbm = pl.BlockSpec(memory_space=pltpu.HBM)
    return pl.pallas_call(
        couple_kernel,
        grid_spec=pltpu.PrefetchScalarGridSpec(
            num_scalar_prefetch=1,
            grid=(),
            in_specs=[hbm] * 2,
            out_specs=pl.BlockSpec(memory_space=pltpu.VMEM),
            scratch_shapes=[
                pltpu.VMEM((ENTRIES, 16, 128), BF16),
                pltpu.VMEM((4 * BLOCKS, 128, 128), BF16),
                pltpu.VMEM((4 * ROWS * RANK, 16), BF16),
                pltpu.VMEM((4 * ROWS, 16, RANK), F32),
                pltpu.SemaphoreType.DMA((2,)),
            ],
        ),
        out_shape=jax.ShapeDtypeStruct((4, PAIRS, 16, 128), BF16),
        compiler_params=pltpu.CompilerParams(vmem_limit_bytes=VMEM_BYTES),
        name="coupling",
    )(lists, table, blocks)


def down_kernel(
    far, basis_in, t_one_in, t_two_in, out, basis, t_one, t_two, came, near, in_sem, send, recv
):
    space = lax.axis_index("space")
    leaf = lax.axis_index("leaf")
    x = leaf // 4
    four = lax.rem(leaf, 4)
    loads = [
        pltpu.make_async_copy(src, dst, in_sem.at[k])
        for k, (src, dst) in enumerate(((t_two_in, t_two), (t_one_in, t_one), (basis_in, basis), (far.at[x], came.at[x])))
    ]
    for load in loads:
        load.start()
    barrier = pltpu.get_barrier_semaphore()
    for k in range(1, 4):
        to = lax.rem(x + k, 4) * 4 + four
        pl.semaphore_signal(barrier, inc=1, device_id=(space, to), device_id_type=MESH)
    pl.semaphore_wait(barrier, 3)

    def copy(k):
        to = lax.rem(x + k, 4)
        return pltpu.make_async_remote_copy(
            src_ref=far.at[to], dst_ref=came.at[x], send_sem=send.at[k], recv_sem=recv.at[x],
            device_id=(space, to * 4 + four), device_id_type=MESH,
        )

    for k in range(1, 4):
        copy(k).start()
    for load in loads:
        load.wait()
    for k in range(1, 4):
        source = lax.rem(x + k, 4)
        pltpu.make_async_remote_copy(
            src_ref=far.at[source], dst_ref=came.at[source], send_sem=send.at[k], recv_sem=recv.at[source],
            device_id=(space, leaf), device_id_type=MESH,
        ).wait_recv()

    def summed(i):
        return (
            came[0, i].astype(F32) + came[1, i].astype(F32)
            + came[2, i].astype(F32) + came[3, i].astype(F32)
        )

    local_two = summed(36)[:, :RANK].astype(BF16)
    down_one = jnp.dot(local_two, t_two[0], preferred_element_type=F32)
    for i in range(4):
        near[32 + i] = (summed(32 + i) + down_one[:, 128 * i : 128 * i + 128]).astype(BF16)

    def cluster(i, carry):
        both = near[32 + i]
        for h in range(2):
            local_one = both[:, h * RANK : (h + 1) * RANK]
            down_leaf = jnp.dot(local_one, t_one[2 * i + h], preferred_element_type=F32)
            for j in range(4):
                pair = 8 * i + 4 * h + j
                local_leaf = (summed(pair) + down_leaf[:, 128 * j : 128 * j + 128]).astype(BF16)
                for s in range(2):
                    at = pl.multiple_of((2 * pair + s) * 128, 128)
                    out[:, pl.ds(at, 128)] = jnp.dot(
                        local_leaf[:, s * RANK : (s + 1) * RANK], basis[2 * pair + s],
                        preferred_element_type=F32,
                    ).astype(BF16)
        return carry

    lax.fori_loop(0, 4, cluster, 0)
    for k in range(1, 4):
        copy(k).wait_send()


def downward(far, basis, t_one, t_two):
    hbm = pl.BlockSpec(memory_space=pltpu.HBM)
    dma = pltpu.SemaphoreType.DMA
    return pl.pallas_call(
        down_kernel,
        out_shape=jax.ShapeDtypeStruct((16, LEAF_DEV * 128), BF16),
        in_specs=[hbm] * 4,
        out_specs=pl.BlockSpec(memory_space=pltpu.VMEM),
        scratch_shapes=[pltpu.VMEM(a.shape, a.dtype) for a in (basis, t_one, t_two)]
        + [
            pltpu.VMEM((4, PAIRS, 16, 128), BF16),
            pltpu.VMEM((36, 16, 128), BF16),
            dma((4,)), dma((4,)), dma((4,)),
        ],
        compiler_params=pltpu.CompilerParams(
            collective_id=1, has_side_effects=True, vmem_limit_bytes=VMEM_BYTES
        ),
        name="downward",
    )(far, basis, t_one, t_two)


def local(
    charges, leaf_basis, transfer_one, transfer_two, nodes_leaf, nodes_one, nodes_two,
    links_leaf, links_one, links_two,
):
    table, blocks, lists = upward(
        lax.axis_size("space"), charges, leaf_basis, transfer_one, transfer_two,
        nodes_leaf.transpose(1, 0, 2), nodes_one.transpose(1, 0, 2), nodes_two.reshape(3, RANK),
        links_leaf, links_one, links_two,
    )
    far = coupling(lists.reshape(4 * ROWS, 128), table, blocks)
    return downward(far, leaf_basis, transfer_one, transfer_two)


def solution(mesh):
    return jax.shard_map(
        local,
        mesh=mesh,
        in_specs=(
            P(None, ("space", "leaf")),
            P(("space", "leaf"), None, None),
            P(("space", "leaf"), None, None),
            P(("space", "leaf"), None, None),
            P(("space", "leaf"), None, None),
            P(("space", "leaf"), None, None),
            P(("space", "leaf"), None, None),
            P(("space", "leaf"), None),
            P(("space", "leaf"), None),
            P(("space", "leaf"), None),
        ),
        out_specs=P(None, ("space", "leaf")),
        check_vma=False,
    )
```

time: 111 us -> 98.5 us (0.89)
  local copies, waits for them, and re-layouts: 7.14 us -> 1.67 us
  Pallas kernels: 100 us -> 95.7 us
  other arithmetic: 3.07 us -> 0 us
    pallas_call x1, Pallas kernels: 57 us -> 44.6 us  [coupling(): pl.pallas_call(couple_kernel, grid_spec=pltpu.PrefetchScalarGridSpec(num_...]
    pallas_call x1, Pallas kernels: 30.5 us -> 36.3 us  [upward(): pl.pallas_call(functools.partial(up_kernel, n_space), out_shape=(jax.Shap...]
    unnamed x15 -> x1, local copies, waits for them, and re-layouts: 4.77 us -> 1.67 us
    reshape x4 -> x0, local copies, waits for them, and re-layouts: 2.36 us -> none  [packed_nodes(): rows.append(flat.reshape(3, -1, 128))]
    pallas_call x1, Pallas kernels: 12.5 us -> 14.8 us  [downward(): pl.pallas_call(down_kernel, out_shape=jax.ShapeDtypeStruct((16, LEAF_DEV...]
    add x3 -> x0, other arithmetic: 2.25 us -> none  [the longest x2 1.58 us: near(): return owner // 4 % 4 * 1024 + slot * SLOT + offset + links % per_dev]
where the time goes in v2:
time: 98.5 us; the launch traced here: 97.4 us
  Pallas kernels  95.7 us (97%)
  local copies, waits for them, and re-layouts  1.67 us (2%)
    pallas_call x1, Pallas kernels, coupling(): pl.pallas_call(couple_kernel, grid_spec=pltpu.PrefetchScalarGridSpec(num_...  44.6 us
    pallas_call x1, Pallas kernels, upward(): pl.pallas_call(functools.partial(up_kernel, n_space), out_shape=(jax.Shap...  36.3 us
    pallas_call x1, Pallas kernels, downward(): pl.pallas_call(down_kernel, out_shape=jax.ShapeDtypeStruct((16, LEAF_DEV...  14.8 us

profile of v2, /device:TPU:32, one launch (start us, length us, event | category | flops | bytes accessed | tf_op | source)
XLA Modules:
  0.0 97.4 jit_solution(18267996133906220271)
XLA Ops:
  0.0 36.3 %upward.1 = (bf16[936,16,128]{2,1,0:T(8,128)(2,1)}, bf16[20,128,128]{2,1,0:T(8,128)(2,1)}, s32[4,80,128]{2,1,0:T(8,128)}) custom-call(bf16[16,8192]{1,0:T(8,128)(2,1)} %charges_in.1, bf16[64,64,128]{2,1,0:T(8,128)(2,1)} %basis_in.3, bf16[8,64,512]{2,1,0:T(8,128)(2,1)} %t_one_in.3, bf16[1,64,512]{2,1,0:T(8,128)(2,1)} %t_two_in.3, bf16[3,64,64]{2,1,0:T(8,128)(2,1)} %bitcast.5, ...), custom_call_target="tpu_custom_call" | custom-call | tf_op jit(solution)/shard_map/upward/pallas_call | solution.py:466
  36.3 44.6 %coupling.1.far = bf16[4,37,16,128]{3,2,1,0:T(8,128)(2,1)} custom-call(s32[320,128]{1,0:T(8,128)} %bitcast.4, bf16[936,16,128]{2,1,0:T(8,128)(2,1)} %get-tuple-element.9.table_in, bf16[20,128,128]{2,1,0:T(8,128)(2,1)} %get-tuple-element.10.blocks_in), custom_call_target="tpu_custom_call" | custom-call | tf_op jit(solution)/shard_map/coupling/pallas_call | solution.py:567
  80.9 14.8 %downward.1 = bf16[16,8192]{1,0:T(8,128)(2,1)} custom-call(bf16[4,37,16,128]{3,2,1,0:T(8,128)(2,1)} %coupling.1.far, bf16[64,64,128]{2,1,0:T(8,128)(2,1)} %basis_in.3, bf16[8,64,512]{2,1,0:T(8,128)(2,1)} %t_one_in.3, bf16[1,64,512]{2,1,0:T(8,128)(2,1)} %t_two_in.3), custom_call_target="tpu_custom_call" | custom-call | tf_op jit(solution)/shard_map/downward/pallas_call | solution.py:660
  95.7 1.7 %copy.12 = bf16[16,8192]{1,0:T(8,128)(2,1)} copy(bf16[16,8192]{1,0:T(8,128)(2,1)} %downward.1) | data formatting | bytes 524288

commit v3 on v2

--- a/solution.py
+++ b/solution.py
@@ -30,6 +30,7 @@
 CUT = 16
 BLOCKS = 5
 VMEM_BYTES = 58 * 1024 * 1024
+DOWN_BYTES = 53 * 1024 * 1024 + 512 * 1024
 
 
 def nt(a, b):
@@ -225,9 +226,6 @@
             stacked = jnp.concatenate([coef[4 * p + j] for j in range(4)], axis=1)
             halves.append(nt(stacked, t_one[p]))
         coef[32 + i] = jnp.concatenate(halves, axis=1).astype(BF16)
-    send_all(2)
-    pass_ab(0)
-
     loads[6].wait()
     top = nt(jnp.concatenate([coef[32 + j] for j in range(4)], axis=1), t_two[0])
     tx, ty, tz = (nodes_f[c * PLANE + 36 : c * PLANE + 37, 0:RANK] for c in range(3))
@@ -248,7 +246,10 @@
 
     for k in range(1, n_space):
         two_copy(k).start()
+    send_all(2)
     two_tab[own_two] = entry[...]
+    pass_ab(0)
+    pass_ab(1)
 
     for load in loads[7:]:
         load.wait()
@@ -284,7 +285,6 @@
     lane_f = lane.astype(F32)
     for q in range(4):
         packed[q] = jnp.broadcast_to(jnp.maximum((counts[q].astype(jnp.int32) + 3) // 4, 1), (ROWS, 128))
-    pass_ab(1)
 
     def compact(b, carry):
         block = pl.ds(pl.multiple_of(b * 8, 8), 8)
@@ -300,16 +300,16 @@
             packed[q, block, :] = jnp.where(lane == 127, packed[q, block, :], found[q].astype(jnp.int32))
         return carry
 
-    lax.fori_loop(0, ROWS // 8, compact, 0)
+    lax.fori_loop(0, 4, compact, 0)
+    pass_ab(2)
+    lax.fori_loop(4, ROWS // 8, compact, 0)
     for k in range(1, 4):
         to = lax.rem(x + k, 4)
         remote(packed.at[to], lists.at[x], send_l.at[k], recv_l.at[x], space, to * 4 + four).start()
     keep_list = pltpu.make_async_copy(packed.at[x], lists.at[x], local_sem)
     keep_list.start()
     pass_c(0)
-    pass_ab(2)
     pass_c(1)
-    pass_z(0)
 
     def planes(source):
         px, py, pz = (source[c * PLANE : (c + 1) * PLANE, :].astype(F32) for c in range(3))
@@ -332,15 +332,15 @@
             feat[pl.ds(k, PLANE, stride=16), :] = part
 
         def some(b, carry):
-            for j in range(6):
-                i = b * 6 + j
+            for j in range(12):
+                i = b * 12 + j
                 f = feat[pl.ds(pl.multiple_of(i * 16, 16), 16), :].astype(BF16)
                 c = coefs(i)
                 table[slot * SLOT + 2 * i] = jnp.concatenate([f[:, :RANK], c[:, :RANK]], axis=1)
                 table[slot * SLOT + 2 * i + 1] = jnp.concatenate([f[:, RANK:], c[:, RANK:]], axis=1)
             return carry
 
-        lax.fori_loop(0, 6, some, 0)
+        lax.fori_loop(0, 3, some, 0)
         table_copy(slot).start()
 
     def enter_held(slot):
@@ -356,12 +356,11 @@
         for b in range(BLOCKS):
             blocks[which * BLOCKS + b] = feat_t[b * 128 : (b + 1) * 128, :].T.astype(BF16)
 
-    aim(x, nodes)
-    pass_c(2)
-    pass_z(1)
     enter(mine, nodes, lambda i: coef[i])
     table[pl.ds(ZERO_AT, 8)] = jnp.zeros((8, 16, 128), BF16)
-    pass_z(2)
+    pass_c(2)
+    pass_z(0)
+    pass_z(1)
 
     for k in range(1, n_space):
         source = lax.rem(space + k, n_space)
@@ -381,17 +380,19 @@
 
     band_copy(0).start()
     band_copy(1).start()
-
+    for slot in (slot_a, slot_b):
+        enter_held(slot)
+    pass_z(2)
+    band_arrived(four_y)
+    band_copy(2).start()
+    aim(x, nodes)
     for k in range(1, 4):
         source = lax.rem(x + k, 4)
         remote(nodes, target_nodes.at[source], send_x.at[k], recv_x.at[source], space, leaf).wait_recv()
         aim(source, target_nodes.at[source])
-
-    band_arrived(four_y)
-    band_copy(2).start()
-
-    for slot in (slot_a, slot_b, slot_c):
-        enter_held(slot)
+    blocks_copy = pltpu.make_async_copy(blocks, blocks_out, out_sem.at[13])
+    blocks_copy.start()
+    enter_held(slot_c)
 
     def from_sibling(slot):
         for piece in range(PIECES):
@@ -412,12 +413,8 @@
     band_arrived(beside_y)
     table[pl.ds(TWO_AT, 64)] = two_tab[...]
     rest = pl.ds(TWO_AT, ENTRIES - TWO_AT)
-    ends = (
-        pltpu.make_async_copy(table.at[rest], table_out.at[rest], out_sem.at[12]),
-        pltpu.make_async_copy(blocks, blocks_out, out_sem.at[13]),
-    )
-    for copy in ends:
-        copy.start()
+    rest_copy = pltpu.make_async_copy(table.at[rest], table_out.at[rest], out_sem.at[12])
+    rest_copy.start()
     for k in range(1, 4):
         source = lax.rem(x + k, 4)
         remote(packed.at[0], lists.at[source], send_l.at[k], recv_l.at[source], space, leaf).wait_recv()
@@ -456,8 +453,8 @@
         for slot in slot_z + (far + beside_y, far + beside):
             table_copy(slot).wait()
 
-    for copy in ends:
-        copy.wait()
+    rest_copy.wait()
+    blocks_copy.wait()
 
 
 def upward(n_space, *arrays):
@@ -520,14 +517,15 @@
     lax.fori_loop(0, 4 * ROWS // 16, clear, 0)
     loads[0].wait()
 
-    def spread(b, carry):
-        block = blocks[b]
-        for j in range(8):
-            start = pl.multiple_of((b * 8 + j) * 128, 128)
-            targets[pl.ds(start, 128), :] = block[:, 16 * j : 16 * j + 16]
+    def spread(q, carry):
+        for i in range(BLOCKS):
+            block = blocks[q * BLOCKS + i]
+            for j in range(8):
+                start = pl.multiple_of(((q * BLOCKS + i) * 8 + j) * 128, 128)
+                targets[pl.ds(start, 128), :] = block[:, 16 * j : 16 * j + 16]
         return carry
 
-    lax.fori_loop(0, 4 * BLOCKS, spread, 0)
+    lax.fori_loop(0, 4, spread, 0)
     loads[1].wait()
 
     end = 4 * ROWS - 1
@@ -552,14 +550,14 @@
 
     lax.while_loop(lambda c: c[0] < end, step, (jnp.int32(0), jnp.int32(0), jnp.int32(0)))
 
-    def pack(i, carry):
-        for q in range(4):
+    def pack(q, carry):
+        for i in range(PAIRS):
             at = q * ROWS + 2 * i
             both = jnp.concatenate([total[at], total[at + 1]], axis=1)
             out[q, i] = (both * (AMPLITUDE * SCALE)).astype(BF16)
         return carry
 
-    lax.fori_loop(0, PAIRS, pack, 0)
+    lax.fori_loop(0, 4, pack, 0)
 
 
 def coupling(lists, table, blocks):
@@ -669,7 +667,7 @@
             dma((4,)), dma((4,)), dma((4,)),
         ],
         compiler_params=pltpu.CompilerParams(
-            collective_id=1, has_side_effects=True, vmem_limit_bytes=VMEM_BYTES
+            collective_id=1, has_side_effects=True, vmem_limit_bytes=DOWN_BYTES
         ),
         name="downward",
     )(far, basis, t_one, t_two)

time: 98.5 us -> 87.2 us (0.89)
  the two profiles are of different devices: /device:TPU:32 before, /device:TPU:105 now
where the time goes in v3:
time: 87.2 us; the launch traced here: 87 us
  Pallas kernels  86.3 us (99%)
    pallas_call x1, Pallas kernels, coupling(): pl.pallas_call(couple_kernel, grid_spec=pltpu.PrefetchScalarGridSpec(num_...  45.6 us
    pallas_call x1, Pallas kernels, upward(): pl.pallas_call(functools.partial(up_kernel, n_space), out_shape=(jax.Shap...  27.2 us
    pallas_call x1, Pallas kernels, downward(): pl.pallas_call(down_kernel, out_shape=jax.ShapeDtypeStruct((16, LEAF_DEV...  13.5 us

profile of v3, /device:TPU:105, one launch (start us, length us, event | category | flops | bytes accessed | tf_op | source)
XLA Modules:
  0.0 87.0 jit_solution(11247595120057448506)
XLA Ops:
  0.0 0.0 copy-start
  0.0 27.2 %upward.1 = (bf16[936,16,128]{2,1,0:T(8,128)(2,1)}, bf16[20,128,128]{2,1,0:T(8,128)(2,1)}, s32[4,80,128]{2,1,0:T(8,128)}) custom-call(bf16[16,8192]{1,0:T(8,128)(2,1)} %charges_in.1, bf16[64,64,128]{2,1,0:T(8,128)(2,1)} %basis_in.3, bf16[8,64,512]{2,1,0:T(8,128)(2,1)} %t_one_in.3, bf16[1,64,512]{2,1,0:T(8,128)(2,1)} %t_two_in.3, bf16[3,64,64]{2,1,0:T(8,128)(2,1)} %bitcast.5, ...), custom_call_target="tpu_custom_call" | custom-call | tf_op jit(solution)/shard_map/upward/pallas_call | solution.py:463
  27.3 45.6 %coupling.1.far = bf16[4,37,16,128]{3,2,1,0:T(8,128)(2,1)} custom-call(s32[320,128]{1,0:T(8,128)} %bitcast.4, bf16[936,16,128]{2,1,0:T(8,128)(2,1)} %get-tuple-element.9.table_in, bf16[20,128,128]{2,1,0:T(8,128)(2,1)} %get-tuple-element.10.blocks_in), custom_call_target="tpu_custom_call" | custom-call | tf_op jit(solution)/shard_map/coupling/pallas_call | solution.py:565
  72.9 0.0 copy-done
  72.9 13.5 %downward.1 = bf16[16,8192]{1,0:T(8,128)(2,1)S(1)} custom-call(bf16[4,37,16,128]{3,2,1,0:T(8,128)(2,1)} %coupling.1.far, bf16[64,64,128]{2,1,0:T(8,128)(2,1)} %basis_in.3, bf16[8,64,512]{2,1,0:T(8,128)(2,1)} %t_one_in.3, bf16[1,64,512]{2,1,0:T(8,128)(2,1)S(1)} %copy-done), custom_call_target="tpu_custom_call" | custom-call | tf_op jit(solution)/shard_map/downward/pallas_call | solution.py:658
  86.3 0.7 copy.12
Async XLA Ops:
  0.0 72.9 %copy-start = (bf16[1,64,512]{2,1,0:T(8,128)(2,1)S(1)}, bf16[1,64,512]{2,1,0:T(8,128)(2,1)}, u32[]{:S(2)}) copy-start(bf16[1,64,512]{2,1,0:T(8,128)(2,1)} %t_two_in.3) | copy-start | bytes 196612

commit v4 on v3

--- a/solution.py
+++ b/solution.py
@@ -19,7 +19,11 @@
 ONE_DEV = 8
 PAIRS = 37
 PLANE = 48
-ROWS = 80
+CLASS_ROWS = 24
+CLASS_PAIRS = 10
+ROWS = 4 * CLASS_ROWS
+HOMES = 16
+ALL_ROWS = HOMES * CLASS_ROWS
 SLOT = 72
 TWO_AT = 12 * SLOT
 ZERO_AT = TWO_AT + 64
@@ -28,13 +32,21 @@
 
 PIECES = 3
 CUT = 16
-BLOCKS = 5
+BLOCKS = 2
 VMEM_BYTES = 58 * 1024 * 1024
 DOWN_BYTES = 53 * 1024 * 1024 + 512 * 1024
 
 
 def nt(a, b):
     return lax.dot_general(a, b, (((1,), (1,)), ((), ())), preferred_element_type=F32)
+
+
+def other_four(y_lo, core, kind):
+    return (1 - y_lo if kind >= 2 else y_lo) * 2 + (1 - core if kind % 2 else core)
+
+
+def block_peers():
+    return [(k, kind) for k in range(4) for kind in range(4) if (k, kind) != (0, 0)]
 
 
 def split3(value):
@@ -50,7 +62,7 @@
     leaf_links_in, one_links_in, two_links_in,
     table_out, blocks_out, lists,
     charges, basis, t_one, t_two, leaf_nodes, one_nodes, two_nodes, leaf_links, one_links, two_links,
-    nodes_f, nodes, coef, entry, packed, order, value, feat, feat_t,
+    nodes_f, nodes, nodes_t, coef, entry, packed, order, value, feat, feat_t,
     node_tab, coef_tab, two_tab, target_nodes, table, blocks,
     in_sem, out_sem, local_sem, send_own, send_relay, send_z, send_sib, recv,
     send_e, recv_e, send_b, recv_b, send_x, recv_x, send_l, recv_l,
@@ -92,13 +104,14 @@
     def greet(s, l):
         pl.semaphore_signal(barrier, inc=1, device_id=(s, l), device_id_type=MESH)
 
-    for k in range(1, 4):
-        greet(space, lax.rem(x + k, 4) * 4 + four)
+    def block_peer(k, kind):
+        return lax.rem(x + k, 4) * 4 + other_four(y_lo, core, kind)
+
+    for k, kind in block_peers():
+        greet(space, block_peer(k, kind))
     for k in range(1, n_space):
         greet(lax.rem(space + k, n_space), leaf)
-    greet(space, other_y)
     greet(plane, other_y)
-    greet(space, sibling)
 
     nodes_f[...] = jnp.zeros((3 * PLANE, 128), F32)
     for load in loads[:3]:
@@ -111,6 +124,17 @@
             nodes_f[base : base + 36, h * RANK : (h + 1) * RANK] = value[pl.ds(h, 36, stride=2), 0:RANK]
         nodes_f[base + 36 : base + 37, 0:RANK] = two_nodes[c : c + 1].astype(F32)
     nodes[...] = nodes_f[...].astype(BF16)
+    for kind in range(4):
+        pieces = []
+        for c in range(3):
+            base = c * PLANE
+            pieces += [
+                nodes_f[base + 8 * kind : base + 8 * kind + 8, :],
+                nodes_f[base + 32 + kind : base + 33 + kind, :],
+                nodes_f[base + 36 : base + 37, :] if kind == 0 else jnp.zeros((1, 128), F32),
+                jnp.zeros((6, 128), F32),
+            ]
+        nodes_t[kind] = jnp.concatenate(pieces, axis=0).astype(BF16)
 
     def remote(src, dst, send, came, s, l):
         return pltpu.make_async_remote_copy(
@@ -207,11 +231,18 @@
             coef[pair] = jnp.concatenate(halves, axis=1).astype(BF16)
         return carry
 
-    pl.semaphore_wait(barrier, 3 + (n_space - 1) + 3)
+    pl.semaphore_wait(barrier, 15 + (n_space - 1) + 1)
     send_all(0)
-    for k in range(1, 4):
-        to = lax.rem(x + k, 4) * 4 + four
-        remote(nodes, target_nodes.at[x], send_x.at[k], recv_x.at[x], space, to).start()
+
+    def target_copy(k, kind):
+        home = x * 4 + kind
+        return remote(
+            nodes_t.at[kind], target_nodes.at[home], send_x.at[k * 4 + kind], recv_x.at[home],
+            space, block_peer(k, kind),
+        )
+
+    for k, kind in block_peers():
+        target_copy(k, kind).start()
     loads[3].wait()
     loads[4].wait()
     lax.fori_loop(0, CUT // 4, leaves, 0)
@@ -261,10 +292,14 @@
         return jnp.where(links >= 0, coded, 4096)
 
     packed[0] = jnp.full((ROWS, 128), 4096, jnp.int32)
-    packed[0, 0:64, 0:96] = code(leaf_links[...], LEAF_DEV, 0)
-    packed[0, 64:72, 0:96] = code(one_links[...], ONE_DEV, LEAF_DEV)
+    leaf_codes = code(leaf_links[...], LEAF_DEV, 0)
+    one_codes = code(one_links[...], ONE_DEV, LEAF_DEV)
+    for kind in range(4):
+        start = kind * CLASS_ROWS
+        packed[0, start : start + 16, 0:96] = leaf_codes[16 * kind : 16 * kind + 16]
+        packed[0, start + 16 : start + 18, 0:96] = one_codes[2 * kind : 2 * kind + 2]
     two = two_links[...]
-    packed[0, 72:73, 0:96] = jnp.where(
+    packed[0, 18:19, 0:96] = jnp.where(
         two >= 0, two // 4 % 4 * 1024 + TWO_AT + two % 4 * 16 + two // 16, 4096
     )
     codes = packed[0]
@@ -300,19 +335,26 @@
             packed[q, block, :] = jnp.where(lane == 127, packed[q, block, :], found[q].astype(jnp.int32))
         return carry
 
-    lax.fori_loop(0, 4, compact, 0)
+    lax.fori_loop(0, 5, compact, 0)
     pass_ab(2)
-    lax.fori_loop(4, ROWS // 8, compact, 0)
-    for k in range(1, 4):
-        to = lax.rem(x + k, 4)
-        remote(packed.at[to], lists.at[x], send_l.at[k], recv_l.at[x], space, to * 4 + four).start()
-    keep_list = pltpu.make_async_copy(packed.at[x], lists.at[x], local_sem)
+    lax.fori_loop(5, ROWS // 8, compact, 0)
+
+    def list_copy(k, kind):
+        home = x * 4 + kind
+        return remote(
+            packed.at[lax.rem(x + k, 4), pl.ds(kind * CLASS_ROWS, CLASS_ROWS)], lists.at[home],
+            send_l.at[k * 4 + kind], recv_l.at[home], space, block_peer(k, kind),
+        )
+
+    for k, kind in block_peers():
+        list_copy(k, kind).start()
+    keep_list = pltpu.make_async_copy(packed.at[x, pl.ds(0, CLASS_ROWS)], lists.at[x * 4], local_sem)
     keep_list.start()
     pass_c(0)
     pass_c(1)
 
-    def planes(source):
-        px, py, pz = (source[c * PLANE : (c + 1) * PLANE, :].astype(F32) for c in range(3))
+    def planes(source, size):
+        px, py, pz = (source[c * size : (c + 1) * size, :].astype(F32) for c in range(3))
         return px, py, pz, split3(px * px + py * py + pz * pz)
 
     ones = jnp.ones((PLANE, 128), F32)
@@ -320,14 +362,14 @@
     for k in range(6, 16):
         feat[pl.ds(k, PLANE, stride=16), :] = ones if k < 9 else zeros
     for k in range(3, 16):
-        feat_t[pl.ds(k, PLANE, stride=16), :] = ones if k < 6 else zeros
+        feat_t[pl.ds(k, 16, stride=16), :] = (ones if k < 6 else zeros)[:16]
 
     def table_copy(slot):
         part = pl.ds(slot * SLOT, SLOT)
         return pltpu.make_async_copy(table.at[part], table_out.at[part], out_sem.at[slot])
 
     def enter(slot, source, coefs):
-        px, py, pz, norm = planes(source)
+        px, py, pz, norm = planes(source, PLANE)
         for k, part in enumerate((px, py, pz) + norm):
             feat[pl.ds(k, PLANE, stride=16), :] = part
 
@@ -347,11 +389,11 @@
         enter(slot, node_tab.at[slot], lambda i: coef_tab[slot, i])
 
     def aim(which, source):
-        px, py, pz, norm = planes(source)
+        px, py, pz, norm = planes(source, 16)
         for k, part in enumerate((-2.0 * px, -2.0 * py, -2.0 * pz)):
-            feat_t[pl.ds(k, PLANE, stride=16), :] = part
+            feat_t[pl.ds(k, 16, stride=16), :] = part
         for k, part in enumerate(norm):
-            feat_t[pl.ds(6 + k, PLANE, stride=16), :] = part
+            feat_t[pl.ds(6 + k, 16, stride=16), :] = part
 
         for b in range(BLOCKS):
             blocks[which * BLOCKS + b] = feat_t[b * 128 : (b + 1) * 128, :].T.astype(BF16)
@@ -385,11 +427,11 @@
     pass_z(2)
     band_arrived(four_y)
     band_copy(2).start()
-    aim(x, nodes)
-    for k in range(1, 4):
-        source = lax.rem(x + k, 4)
-        remote(nodes, target_nodes.at[source], send_x.at[k], recv_x.at[source], space, leaf).wait_recv()
-        aim(source, target_nodes.at[source])
+    aim(x * 4, nodes_t.at[0])
+    for k, kind in block_peers():
+        home = lax.rem(x + k, 4) * 4 + kind
+        remote(nodes_t.at[0], target_nodes.at[home], send_x.at[0], recv_x.at[home], space, leaf).wait_recv()
+        aim(home, target_nodes.at[home])
     blocks_copy = pltpu.make_async_copy(blocks, blocks_out, out_sem.at[13])
     blocks_copy.start()
     enter_held(slot_c)
@@ -415,9 +457,11 @@
     rest = pl.ds(TWO_AT, ENTRIES - TWO_AT)
     rest_copy = pltpu.make_async_copy(table.at[rest], table_out.at[rest], out_sem.at[12])
     rest_copy.start()
-    for k in range(1, 4):
-        source = lax.rem(x + k, 4)
-        remote(packed.at[0], lists.at[source], send_l.at[k], recv_l.at[source], space, leaf).wait_recv()
+    for k, kind in block_peers():
+        home = lax.rem(x + k, 4) * 4 + kind
+        remote(
+            packed.at[0, pl.ds(0, CLASS_ROWS)], lists.at[home], send_l.at[0], recv_l.at[home], space, leaf
+        ).wait_recv()
 
     for piece in range(PIECES):
         for copy in own_copies(piece):
@@ -440,10 +484,9 @@
         two_copy(k).wait_send()
     for k in range(3):
         band_copy(k).wait_send()
-    for k in range(1, 4):
-        to = lax.rem(x + k, 4)
-        remote(nodes, target_nodes.at[x], send_x.at[k], recv_x.at[x], space, to * 4 + four).wait_send()
-        remote(packed.at[to], lists.at[x], send_l.at[k], recv_l.at[x], space, to * 4 + four).wait_send()
+    for k, kind in block_peers():
+        target_copy(k, kind).wait_send()
+        list_copy(k, kind).wait_send()
     keep_list.wait()
     for slot in (mine, slot_a, slot_b, slot_c, 4 + beside, 4 + beside_y, near + beside_y, near + beside):
         table_copy(slot).wait()
@@ -464,8 +507,8 @@
         functools.partial(up_kernel, n_space),
         out_shape=(
             jax.ShapeDtypeStruct((ENTRIES, 16, 128), BF16),
-            jax.ShapeDtypeStruct((4 * BLOCKS, 128, 128), BF16),
-            jax.ShapeDtypeStruct((4, ROWS, 128), jnp.int32),
+            jax.ShapeDtypeStruct((HOMES * BLOCKS, 128, 128), BF16),
+            jax.ShapeDtypeStruct((HOMES, CLASS_ROWS, 128), jnp.int32),
         ),
         in_specs=[hbm] * len(arrays),
         out_specs=[hbm] * 3,
@@ -473,26 +516,27 @@
         + [
             pltpu.VMEM((3 * PLANE, 128), F32),
             pltpu.VMEM((3 * PLANE, 128), BF16),
+            pltpu.VMEM((4, 48, 128), BF16),
             pltpu.VMEM((PAIRS, 16, 128), BF16),
             pltpu.VMEM((16, 128), BF16),
             pltpu.VMEM((4, ROWS, 128), jnp.int32),
             pltpu.VMEM((ROWS, 128), F32),
             pltpu.VMEM((ROWS, 128), F32),
             pltpu.VMEM((PLANE * 16, 128), F32),
-            pltpu.VMEM((PLANE * 16, 128), F32),
+            pltpu.VMEM((256, 128), F32),
             pltpu.VMEM((12, 3 * PLANE, 128), BF16),
             pltpu.VMEM((12, 36, 16, 128), BF16),
             pltpu.VMEM((64, 16, 128), BF16),
-            pltpu.VMEM((4, 3 * PLANE, 128), BF16),
+            pltpu.VMEM((HOMES, 48, 128), BF16),
             pltpu.VMEM((ENTRIES, 16, 128), BF16),
-            pltpu.VMEM((4 * BLOCKS, 128, 128), BF16),
+            pltpu.VMEM((HOMES * BLOCKS, 128, 128), BF16),
             dma((len(arrays),)), dma((14,)),
             dma,
             dma((PIECES, 3)), dma((PIECES,)), dma((PIECES, 2)), dma((PIECES, 5)), dma((PIECES, 12)),
             dma((16,)), dma((16,)),
             dma((3,)), dma((4,)),
-            dma((4,)), dma((4,)),
-            dma((4,)), dma((4,)),
+            dma((16,)), dma((16,)),
+            dma((16,)), dma((16,)),
         ],
         compiler_params=pltpu.CompilerParams(
             collective_id=0, has_side_effects=True, vmem_limit_bytes=VMEM_BYTES
@@ -514,21 +558,23 @@
             total[i * 16 + j] = jnp.zeros((16, RANK), F32)
         return carry
 
-    lax.fori_loop(0, 4 * ROWS // 16, clear, 0)
+    lax.fori_loop(0, ALL_ROWS // 16, clear, 0)
     loads[0].wait()
 
     def spread(q, carry):
-        for i in range(BLOCKS):
-            block = blocks[q * BLOCKS + i]
-            for j in range(8):
-                start = pl.multiple_of(((q * BLOCKS + i) * 8 + j) * 128, 128)
-                targets[pl.ds(start, 128), :] = block[:, 16 * j : 16 * j + 16]
+        for kind in range(4):
+            home = q * 4 + kind
+            for i in range(CLASS_PAIRS):
+                block = blocks[home * BLOCKS + i // 8]
+                start = pl.multiple_of((home * (CLASS_ROWS // 2) + i) * 128, 128)
+                at = 16 * (i % 8)
+                targets[pl.ds(start, 128), :] = block[:, at : at + 16]
         return carry
 
     lax.fori_loop(0, 4, spread, 0)
     loads[1].wait()
 
-    end = 4 * ROWS - 1
+    end = ALL_ROWS - 1
 
     def step(carry):
         r, t, g = carry
@@ -542,8 +588,8 @@
             matrix = ((dist + 1.0 / SCALE) * jnp.exp2(dist * (-SCALE * LOG2E))).astype(BF16)
             total[r] += nt(coefs, matrix)
             done = g + 1 >= lists[r, 127]
-            over = t == 72
-            r = jnp.where(done, jnp.minimum(jnp.where(over, r + 8, r + 1), end), r)
+            over = t == 18
+            r = jnp.where(done, jnp.minimum(jnp.where(over, r + CLASS_ROWS - 18, r + 1), end), r)
             t = jnp.where(done, jnp.where(over, 0, t + 1), t)
             g = jnp.where(done, 0, g + 1)
         return r, t, g
@@ -551,10 +597,12 @@
     lax.while_loop(lambda c: c[0] < end, step, (jnp.int32(0), jnp.int32(0), jnp.int32(0)))
 
     def pack(q, carry):
-        for i in range(PAIRS):
-            at = q * ROWS + 2 * i
-            both = jnp.concatenate([total[at], total[at + 1]], axis=1)
-            out[q, i] = (both * (AMPLITUDE * SCALE)).astype(BF16)
+        for kind in range(4):
+            home = q * 4 + kind
+            for i in range(CLASS_PAIRS):
+                at = home * CLASS_ROWS + 2 * i
+                both = jnp.concatenate([total[at], total[at + 1]], axis=1)
+                out[home, i] = (both * (AMPLITUDE * SCALE)).astype(BF16)
         return carry
 
     lax.fori_loop(0, 4, pack, 0)
@@ -571,13 +619,13 @@
             out_specs=pl.BlockSpec(memory_space=pltpu.VMEM),
             scratch_shapes=[
                 pltpu.VMEM((ENTRIES, 16, 128), BF16),
-                pltpu.VMEM((4 * BLOCKS, 128, 128), BF16),
-                pltpu.VMEM((4 * ROWS * RANK, 16), BF16),
-                pltpu.VMEM((4 * ROWS, 16, RANK), F32),
+                pltpu.VMEM((HOMES * BLOCKS, 128, 128), BF16),
+                pltpu.VMEM((ALL_ROWS * RANK, 16), BF16),
+                pltpu.VMEM((ALL_ROWS, 16, RANK), F32),
                 pltpu.SemaphoreType.DMA((2,)),
             ],
         ),
-        out_shape=jax.ShapeDtypeStruct((4, PAIRS, 16, 128), BF16),
+        out_shape=jax.ShapeDtypeStruct((HOMES, CLASS_PAIRS, 16, 128), BF16),
         compiler_params=pltpu.CompilerParams(vmem_limit_bytes=VMEM_BYTES),
         name="coupling",
     )(lists, table, blocks)
@@ -590,46 +638,53 @@
     leaf = lax.axis_index("leaf")
     x = leaf // 4
     four = lax.rem(leaf, 4)
+    y_lo = four // 2
+    core = lax.rem(four, 2)
     loads = [
         pltpu.make_async_copy(src, dst, in_sem.at[k])
-        for k, (src, dst) in enumerate(((t_two_in, t_two), (t_one_in, t_one), (basis_in, basis), (far.at[x], came.at[x])))
+        for k, (src, dst) in enumerate(
+            ((t_two_in, t_two), (t_one_in, t_one), (basis_in, basis), (far.at[x * 4], came.at[0, x]))
+        )
     ]
     for load in loads:
         load.start()
+
+    def peer(k, kind):
+        return lax.rem(x + k, 4) * 4 + other_four(y_lo, core, kind)
+
     barrier = pltpu.get_barrier_semaphore()
-    for k in range(1, 4):
-        to = lax.rem(x + k, 4) * 4 + four
-        pl.semaphore_signal(barrier, inc=1, device_id=(space, to), device_id_type=MESH)
-    pl.semaphore_wait(barrier, 3)
-
-    def copy(k):
-        to = lax.rem(x + k, 4)
+    for k, kind in block_peers():
+        pl.semaphore_signal(barrier, inc=1, device_id=(space, peer(k, kind)), device_id_type=MESH)
+    pl.semaphore_wait(barrier, 15)
+
+    def copy(k, kind):
+        home = lax.rem(x + k, 4) * 4 + kind
         return pltpu.make_async_remote_copy(
-            src_ref=far.at[to], dst_ref=came.at[x], send_sem=send.at[k], recv_sem=recv.at[x],
-            device_id=(space, to * 4 + four), device_id_type=MESH,
-        )
-
-    for k in range(1, 4):
-        copy(k).start()
+            src_ref=far.at[home], dst_ref=came.at[kind, x], send_sem=send.at[k * 4 + kind],
+            recv_sem=recv.at[kind * 4 + x], device_id=(space, peer(k, kind)), device_id_type=MESH,
+        )
+
+    for k, kind in block_peers():
+        copy(k, kind).start()
     for load in loads:
         load.wait()
-    for k in range(1, 4):
+    for k, kind in block_peers():
         source = lax.rem(x + k, 4)
         pltpu.make_async_remote_copy(
-            src_ref=far.at[source], dst_ref=came.at[source], send_sem=send.at[k], recv_sem=recv.at[source],
-            device_id=(space, leaf), device_id_type=MESH,
+            src_ref=far.at[0], dst_ref=came.at[kind, source], send_sem=send.at[0],
+            recv_sem=recv.at[kind * 4 + source], device_id=(space, leaf), device_id_type=MESH,
         ).wait_recv()
 
-    def summed(i):
+    def summed(kind, i):
         return (
-            came[0, i].astype(F32) + came[1, i].astype(F32)
-            + came[2, i].astype(F32) + came[3, i].astype(F32)
-        )
-
-    local_two = summed(36)[:, :RANK].astype(BF16)
+            came[kind, 0, i].astype(F32) + came[kind, 1, i].astype(F32)
+            + came[kind, 2, i].astype(F32) + came[kind, 3, i].astype(F32)
+        )
+
+    local_two = summed(0, 9)[:, :RANK].astype(BF16)
     down_one = jnp.dot(local_two, t_two[0], preferred_element_type=F32)
     for i in range(4):
-        near[32 + i] = (summed(32 + i) + down_one[:, 128 * i : 128 * i + 128]).astype(BF16)
+        near[32 + i] = (summed(i, 8) + down_one[:, 128 * i : 128 * i + 128]).astype(BF16)
 
     def cluster(i, carry):
         both = near[32 + i]
@@ -638,7 +693,7 @@
             down_leaf = jnp.dot(local_one, t_one[2 * i + h], preferred_element_type=F32)
             for j in range(4):
                 pair = 8 * i + 4 * h + j
-                local_leaf = (summed(pair) + down_leaf[:, 128 * j : 128 * j + 128]).astype(BF16)
+                local_leaf = (summed(i, 4 * h + j) + down_leaf[:, 128 * j : 128 * j + 128]).astype(BF16)
                 for s in range(2):
                     at = pl.multiple_of((2 * pair + s) * 128, 128)
                     out[:, pl.ds(at, 128)] = jnp.dot(
@@ -648,8 +703,8 @@
         return carry
 
     lax.fori_loop(0, 4, cluster, 0)
-    for k in range(1, 4):
-        copy(k).wait_send()
+    for k, kind in block_peers():
+        copy(k, kind).wait_send()
 
 
 def downward(far, basis, t_one, t_two):
@@ -662,9 +717,9 @@
         out_specs=pl.BlockSpec(memory_space=pltpu.VMEM),
         scratch_shapes=[pltpu.VMEM(a.shape, a.dtype) for a in (basis, t_one, t_two)]
         + [
-            pltpu.VMEM((4, PAIRS, 16, 128), BF16),
+            pltpu.VMEM((4, 4, CLASS_PAIRS, 16, 128), BF16),
             pltpu.VMEM((36, 16, 128), BF16),
-            dma((4,)), dma((4,)), dma((4,)),
+            dma((4,)), dma((16,)), dma((16,)),
         ],
         compiler_params=pltpu.CompilerParams(
             collective_id=1, has_side_effects=True, vmem_limit_bytes=DOWN_BYTES
@@ -682,7 +737,7 @@
         nodes_leaf.transpose(1, 0, 2), nodes_one.transpose(1, 0, 2), nodes_two.reshape(3, RANK),
         links_leaf, links_one, links_two,
     )
-    far = coupling(lists.reshape(4 * ROWS, 128), table, blocks)
+    far = coupling(lists.reshape(ALL_ROWS, 128), table, blocks)
     return downward(far, leaf_basis, transfer_one, transfer_two)
 
 

time: 87.2 us -> 94.2 us (1.080)
  the two profiles are of different devices: /device:TPU:105 before, /device:TPU:32 now
where the time goes in v4:
time: 94.2 us; the launch traced here: 93.2 us
  Pallas kernels  92.4 us (98%)
    pallas_call x1, Pallas kernels, coupling(): pl.pallas_call(couple_kernel, grid_spec=pltpu.PrefetchScalarGridSpec(num_...  39.6 us
    pallas_call x1, Pallas kernels, upward(): pl.pallas_call(functools.partial(up_kernel, n_space), out_shape=(jax.Shap...  36.6 us
    pallas_call x1, Pallas kernels, downward(): pl.pallas_call(down_kernel, out_shape=jax.ShapeDtypeStruct((16, LEAF_DEV...  16.3 us

profile of v4, /device:TPU:32, one launch (start us, length us, event | category | flops | bytes accessed | tf_op | source)
XLA Modules:
  0.0 93.2 jit_solution(3524449393256165345)
XLA Ops:
  0.0 0.0 copy-start
  0.0 36.6 %upward.1 = (bf16[936,16,128]{2,1,0:T(8,128)(2,1)}, bf16[32,128,128]{2,1,0:T(8,128)(2,1)}, s32[16,24,128]{2,1,0:T(8,128)}) custom-call(bf16[16,8192]{1,0:T(8,128)(2,1)} %charges_in.1, bf16[64,64,128]{2,1,0:T(8,128)(2,1)} %basis_in.3, bf16[8,64,512]{2,1,0:T(8,128)(2,1)} %t_one_in.3, bf16[1,64,512]{2,1,0:T(8,128)(2,1)} %t_two_in.3, ...), custom_call_target="tpu_custom_call" | custom-call | tf_op jit(solution)/shard_map/upward/pallas_call | solution.py:506
  36.6 39.6 %coupling.1.far = bf16[16,10,16,128]{3,2,1,0:T(8,128)(2,1)} custom-call(s32[384,128]{1,0:T(8,128)} %bitcast.4, bf16[936,16,128]{2,1,0:T(8,128)(2,1)} %get-tuple-element.9.table_in, bf16[32,128,128]{2,1,0:T(8,128)(2,1)} %get-tuple-element.10.blocks_in), custom_call_target="tpu_custom_call" | custom-call | tf_op jit(solution)/shard_map/coupling/pallas_call | solution.py:613
  76.1 0.0 copy-done
  76.2 16.3 %downward.1 = bf16[16,8192]{1,0:T(8,128)(2,1)S(1)} custom-call(bf16[16,10,16,128]{3,2,1,0:T(8,128)(2,1)} %coupling.1.far, bf16[64,64,128]{2,1,0:T(8,128)(2,1)} %basis_in.3, bf16[8,64,512]{2,1,0:T(8,128)(2,1)} %t_one_in.3, bf16[1,64,512]{2,1,0:T(8,128)(2,1)S(1)} %copy-done), custom_call_target="tpu_custom_call" | custom-call | tf_op jit(solution)/shard_map/downward/pallas_call | solution.py:713
  92.5 0.7 copy.12
Async XLA Ops:
  0.0 76.1 %copy-start = (bf16[1,64,512]{2,1,0:T(8,128)(2,1)S(1)}, bf16[1,64,512]{2,1,0:T(8,128)(2,1)}, u32[]{:S(2)}) copy-start(bf16[1,64,512]{2,1,0:T(8,128)(2,1)} %t_two_in.3) | copy-start | bytes 196612
